TPU v7x, 1024 devices: a whole 4x8x16 slice. The times are simulated.
1024 devices in a mesh: gx: 8 (over x, core), gy: 32 (over z_lo, y), ha: 4 (over z_hi).
Axes of the slice: x: 4, y: 8, z: 16 (z_hi: 4, z_lo: 4; z = z_hi * 4 + z_lo), core: 2. Of those that a mesh axis runs over, the one named last changes fastest.
Arguments:
- global_state: float32 [8, 60, 64, 128], P(None, 'ha', 'gx', 'gy'), may hold values from -6 to 6
- crm_state: float32 [8, 60, 64, 8192], P(None, 'ha', 'gx', 'gy'), may hold values from -6 to 6
- mixing: float32 [8, 8], replicated, may hold values from -2 to 2
- substeps: int32 [64, 128], P('gx', 'gy'), may hold values from 1 to 8
- assignment: int32 [64, 128], P('gx', 'gy'), may hold values from 0 to 31, as said below
Outputs:
- new_global: float32 [8, 60, 64, 128], P(None, 'ha', 'gx', 'gy')
- new_crm: float32 [8, 60, 524288], P(None, None, ('gx', 'gy', 'ha'))
Inputs may be any that keep to these rules, and one draw needn't show every extreme that they name: `assignment`: within each tile of 8 x 4 columns every value 0 .. 31 appears once; value // 8 is the helper index, value % 8 the slot on that helper.
All inputs are finite; a program needn't handle non-finite values.
Results may differ from a plain program's by a relative error of at most 0.0003.
Values sent between devices are 32-bit elements; how exact they have to be, the bound alone decides.
No kernel may reach another device: no remote copies, remote signals or barrier semaphores. Data moves between devices by JAX's collectives and lax.ppermute only.
A program may use at most 64 MiB of HBM per device.

v0:
```python
import jax
import jax.numpy as jnp
from jax import lax
from jax.sharding import PartitionSpec as P

MAXSUB = 8
GSUB = 4


HIGH = lax.Precision.HIGHEST


def extended(cells, sides, width):
    for axis, dim in sides:
        count = lax.axis_size(axis)
        head = lax.slice_in_dim(cells, 0, width, axis=dim)
        tail = lax.slice_in_dim(cells, cells.shape[dim] - width, cells.shape[dim], axis=dim)
        cells = jnp.concatenate(
            [
                lax.ppermute(tail, axis, [(i, (i + 1) % count) for i in range(count)]),
                cells,
                lax.ppermute(head, axis, [((i + 1) % count, i) for i in range(count)]),
            ],
            axis=dim,
        )
    return cells


def global_operator(padded):
    center = padded[:, :, 1:-1, 1:-1]
    east = padded[:, :, 2:, 1:-1]
    west = padded[:, :, :-2, 1:-1]
    north = padded[:, :, 1:-1, 2:]
    south = padded[:, :, 1:-1, :-2]
    return (
        0.2 * (east + west + north + south - 4.0 * center)
        - 0.15 * (east - west)
        - 0.15 * (north - south)
    )


def crm_update(state, pushed, mixing):
    lateral = jnp.roll(state, 1, axis=3) + jnp.roll(state, -1, axis=3) - 2.0 * state
    upper = jnp.concatenate([state[:, :1], state[:, :-1]], axis=1)
    lower = jnp.concatenate([state[:, 1:], state[:, -1:]], axis=1)
    coupling = jnp.einsum("gf,flsc->glsc", mixing, jnp.tanh(state), precision=HIGH)
    return state + 0.1 * (1.0 * lateral + 0.5 * (upper + lower - 2.0 * state) + pushed + coupling)


def advance(states, pushed, slot_counts, mixing):

    def one_step(index, state):
        updated = crm_update(state, pushed, mixing)
        return jnp.where((index < slot_counts)[:, None], updated, state)

    return lax.fori_loop(0, MAXSUB, one_step, states)


def on_device(global_state, crm_state, mixing, substeps, assignment):
    current = global_state
    for substep in range(GSUB // 2):
        padded = extended(current, (("gx", 2), ("gy", 3)), 2)
        middle = padded[:, :, 1:-1, 1:-1] + 0.5 * global_operator(padded)
        current = middle[:, :, 1:-1, 1:-1] + 0.5 * global_operator(middle)
    forcing = (current - global_state) / (0.5 * GSUB)
    tile_x, tile_y = assignment.shape
    columns = tile_x * tile_y
    helpers = lax.axis_size("ha")
    per_helper = columns // helpers
    fields, level_part = (crm_state.shape[0], crm_state.shape[1])
    width = crm_state.shape[3] // tile_y
    global_fields = forcing.shape[0]
    onehot = (
        assignment.reshape(columns)[:, None] == jnp.arange(columns, dtype=jnp.int32)[None, :]
    ).astype(jnp.float32)
    helper = lax.axis_index("ha")
    own_slots = lax.dynamic_slice_in_dim(onehot, helper * per_helper, per_helper, 1)
    local_states = crm_state.reshape(fields, level_part, columns, width)
    slotted = jnp.einsum("flxc,xj->fljc", local_states, onehot, precision=HIGH)
    pushes = jnp.einsum(
        "glx,xj->glj", forcing.reshape(global_fields, level_part, columns), onehot, precision=HIGH
    )
    pushes = pushes.reshape(global_fields, level_part, columns, 1)
    states, pushed = (
        lax.all_to_all(slotted, "ha", split_axis=2, concat_axis=1, tiled=True),
        lax.all_to_all(pushes, "ha", split_axis=2, concat_axis=1, tiled=True),
    )
    slot_counts = jnp.dot(
        substeps.reshape(1, columns).astype(jnp.float32), own_slots, precision=HIGH
    )
    slot_counts = slot_counts.reshape(per_helper).astype(jnp.int32)
    advanced = advance(states, pushed, slot_counts, mixing)
    tendency = jnp.mean(advanced - states, axis=3)
    returned = lax.all_to_all(tendency, "ha", split_axis=1, concat_axis=2, tiled=True)
    placed = jnp.dot(returned.reshape(fields * level_part, columns), onehot.T, precision=HIGH)
    new_global = current + placed.reshape(fields, level_part, tile_x, tile_y)
    levels_all = advanced.shape[1]
    return (new_global, advanced.reshape(fields, levels_all, per_helper * width))


def solution(mesh):
    in_specs = (
        P(None, "ha", "gx", "gy"),
        P(None, "ha", "gx", "gy"),
        P(),
        P("gx", "gy"),
        P("gx", "gy"),
    )
    out_specs = (P(None, "ha", "gx", "gy"), P(None, None, ("gx", "gy", "ha")))
    return jax.shard_map(
        on_device, mesh=mesh, in_specs=in_specs, out_specs=out_specs, check_vma=False
    )
```

profile of v0, /device:TPU:6, one launch (start us, length us, event | category | flops | bytes accessed | tf_op | source)
XLA Modules:
  0.0 204.4 jit_solution(12014458064373109301)
XLA Ops:
  1.6 1.7 collective-permute-start.1
  3.3 1.6 collective-permute-done
  4.9 10.6 %collective-permute-done.1 = f32[8,15,2,4]{1,2,3,0:T(2,128)S(1)} collective-permute-done((f32[8,15,2,4]{1,2,3,0:T(2,128)S(1)}, f32[8,15,2,4]{1,2,3,0:T(2,128)S(1)}, u32[]{:S(2)}, u32[]{:S(2)}) %collective-permute-start.1) | collective-permute-done | bytes 3872 | tf_op jit(solution)/shard_map/ppermute | solution.py:22
  15.6 1.9 collective-permute-start.2
  17.6 7.8 %collective-permute-start.3 = (f32[8,15,12,2]{1,2,3,0:T(8,128)S(1)}, f32[8,15,12,2]{1,2,3,0:T(8,128)S(1)}, u32[]{:S(2)}, u32[]{:S(2)}) collective-permute-start(f32[8,15,12,2]{1,2,3,0:T(8,128)S(1)} %get-tuple-element.152), channel_id=1, source_target_pairs={{4,0},{8,4},{12,8},{16,12},{20,16},{24,20},{28,24},{32,28},{36,32}... | collective-permute-start | bytes 34568 | tf_op jit(solution)/shard_map/ppermute | solution.py:22
  26.4 1.5 collective-permute-done.3
  28.5 2.7 %collective-permute-start.4 = (f32[8,15,2,4]{1,2,3,0:T(2,128)S(1)}, f32[8,15,2,4]{1,2,3,0:T(2,128)S(1)}, u32[]{:S(2)}, u32[]{:S(2)}) collective-permute-start(f32[8,15,2,4]{1,2,3,0:T(2,128)S(1)} %get-tuple-element.153), channel_id=1, source_target_pairs={{0,128},{128,256},{256,384},{384,512},{512,640},{640,768},{768,896... | collective-permute-start | bytes 11528 | tf_op jit(solution)/shard_map/ppermute | solution.py:20
  33.8 1.9 collective-permute-start.6
  35.8 8.3 %collective-permute-start.7 = (f32[8,15,12,2]{1,2,3,0:T(8,128)S(1)}, f32[8,15,12,2]{1,2,3,0:T(8,128)S(1)}, u32[]{:S(2)}, u32[]{:S(2)}) collective-permute-start(f32[8,15,12,2]{1,2,3,0:T(8,128)S(1)} %get-tuple-element.150), channel_id=1, source_target_pairs={{4,0},{8,4},{12,8},{16,12},{20,16},{24,20},{28,24},{32,28},{36,32}... | collective-permute-start | bytes 34568 | tf_op jit(solution)/shard_map/ppermute | solution.py:22
  45.2 1.3 collective-permute-done.7
  48.4 7.8 %all-to-all-start.1 = ((f32[4,1,960]{2,1,0:T(1,128)}), f32[4,1,960]{2,1,0:T(1,128)S(1)}, u32[]{:S(2)}, u32[]{:S(2)}) async-start(f32[4,1,960]{2,1,0:T(1,128)} %reshape.67), calls=%async_computation.1 | async-start | bytes 32768 | tf_op jit(solution)/shard_map/all_to_all | solution.py:86
  56.2 1.1 convolution_bitcast_fusion
  58.5 2.3 %reshape.65 = f32[4,1,61440]{2,1,0:T(1,128)} reshape(f32[32,15,8,64]{3,2,1,0:T(8,128)S(1)} %bitcast.68) | data formatting | bytes 1966080
  60.8 7.9 %all-to-all-done.1 = f32[4,1,960]{2,1,0:T(1,128)S(1)} async-done(((f32[4,1,960]{2,1,0:T(1,128)}), f32[4,1,960]{2,1,0:T(1,128)S(1)}, u32[]{:S(2)}, u32[]{:S(2)}) %all-to-all-start.1) | async-done | bytes 15392 | tf_op jit(solution)/shard_map/all_to_all | solution.py:86
  68.8 4.1 %all-to-all-start = ((f32[4,1,61440]{2,1,0:T(1,128)}), f32[4,1,61440]{2,1,0:T(1,128)S(1)}, u32[]{:S(2)}, u32[]{:S(2)}) async-start(f32[4,1,61440]{2,1,0:T(1,128)} %reshape.65), calls=%async_computation | async-start | bytes 1966080 | tf_op jit(solution)/shard_map/all_to_all | solution.py:85
  75.1 48.6 %all-to-all-done = f32[4,1,61440]{2,1,0:T(1,128)S(1)} async-done(((f32[4,1,61440]{2,1,0:T(1,128)}), f32[4,1,61440]{2,1,0:T(1,128)S(1)}, u32[]{:S(2)}, u32[]{:S(2)}) %all-to-all-start) | async-done | bytes 983072 | tf_op jit(solution)/shard_map/all_to_all | solution.py:85
  123.7 3.5 %reduce = f32[4,61440]{1,0:T(4,128)S(1)} reduce(f32[4,1,61440]{2,1,0:T(1,128)S(1)} %all-to-all-done, f32[]{:T(128)} %broadcast.101), dimensions={1}, to_apply=%all_to_all.37.reduce_sub_computation | reduce | bytes 1966084 | tf_op jit(solution)/shard_map/all_to_all | solution.py:85
  128.6 1.1 copy-done
  129.8 53.0 %while.13 = (s32[]{:T(128)}, f32[8,60,8,64]{3,0,2,1:T(8,128)S(1)}, s32[8]{0:T(128)S(1)}, f32[8,60,8,1]{0,2,1,3:T(8,128)S(1)}, f32[8,8]{1,0:T(8,128)S(1)}, /*index=5*/s32[]{:T(128)}) while((s32[]{:T(128)}, f32[8,60,8,64]{3,0,2,1:T(8,128)S(1)}, s32[8]{0:T(128)S(1)}, f32[8,60,8,1]{0,2,1,3:T(8,128)S(1)}, f32[8,8]{1,0:T(8,128)S(1)}, ...), condition=%wide.region_1.2_spmd, body=%wide.region_0.1_spmd.sunk | while | flops 27525128 | bytes 15744385 | solution.py:56
  132.0 4.4 %add_select_fusion.2 = f32[8,60,8,64]{3,0,2,1:T(8,128)S(1)} fusion(f32[8,60,8,64]{3,0,2,1:T(8,128)S(1)} %copy.145, f32[8,60,8,63]{3,0,2,1:T(8,128)S(1)} %get-tuple-element.196, f32[8,60,8,1]{3,0,2,1:T(8,128)S(1)} %get-tuple-element.197, f32[8,60,8,1]{3,0,2,1:T(8,128)S(1)} %get-tuple-element.198, f32[8,60,8,63]{3,0,2,1:T(8,128)S(1)} %get-tuple-element.199, ...), kind=kOutput, calls=%fused_computation.clone.1 | convolution fusion | flops 27525120 | bytes 5913864 | tf_op jit(solution)/shard_map/while/body/eval_jaxpr/gf,flsc->glsc/dot_general | solution.py:46
  138.6 4.4 %add_select_fusion.2 = f32[8,60,8,64]{3,0,2,1:T(8,128)S(1)} fusion(f32[8,60,8,64]{3,0,2,1:T(8,128)S(1)} %copy.145, f32[8,60,8,63]{3,0,2,1:T(8,128)S(1)} %get-tuple-element.196, f32[8,60,8,1]{3,0,2,1:T(8,128)S(1)} %get-tuple-element.197, f32[8,60,8,1]{3,0,2,1:T(8,128)S(1)} %get-tuple-element.198, f32[8,60,8,63]{3,0,2,1:T(8,128)S(1)} %get-tuple-element.199, ...), kind=kOutput, calls=%fused_computation.clone.1 | convolution fusion | flops 27525120 | bytes 5913864 | tf_op jit(solution)/shard_map/while/body/eval_jaxpr/gf,flsc->glsc/dot_general | solution.py:46
  145.2 4.4 %add_select_fusion.2 = f32[8,60,8,64]{3,0,2,1:T(8,128)S(1)} fusion(f32[8,60,8,64]{3,0,2,1:T(8,128)S(1)} %copy.145, f32[8,60,8,63]{3,0,2,1:T(8,128)S(1)} %get-tuple-element.196, f32[8,60,8,1]{3,0,2,1:T(8,128)S(1)} %get-tuple-element.197, f32[8,60,8,1]{3,0,2,1:T(8,128)S(1)} %get-tuple-element.198, f32[8,60,8,63]{3,0,2,1:T(8,128)S(1)} %get-tuple-element.199, ...), kind=kOutput, calls=%fused_computation.clone.1 | convolution fusion | flops 27525120 | bytes 5913864 | tf_op jit(solution)/shard_map/while/body/eval_jaxpr/gf,flsc->glsc/dot_general | solution.py:46
  151.8 4.4 %add_select_fusion.2 = f32[8,60,8,64]{3,0,2,1:T(8,128)S(1)} fusion(f32[8,60,8,64]{3,0,2,1:T(8,128)S(1)} %copy.145, f32[8,60,8,63]{3,0,2,1:T(8,128)S(1)} %get-tuple-element.196, f32[8,60,8,1]{3,0,2,1:T(8,128)S(1)} %get-tuple-element.197, f32[8,60,8,1]{3,0,2,1:T(8,128)S(1)} %get-tuple-element.198, f32[8,60,8,63]{3,0,2,1:T(8,128)S(1)} %get-tuple-element.199, ...), kind=kOutput, calls=%fused_computation.clone.1 | convolution fusion | flops 27525120 | bytes 5913864 | tf_op jit(solution)/shard_map/while/body/eval_jaxpr/gf,flsc->glsc/dot_general | solution.py:46
  158.5 4.4 %add_select_fusion.2 = f32[8,60,8,64]{3,0,2,1:T(8,128)S(1)} fusion(f32[8,60,8,64]{3,0,2,1:T(8,128)S(1)} %copy.145, f32[8,60,8,63]{3,0,2,1:T(8,128)S(1)} %get-tuple-element.196, f32[8,60,8,1]{3,0,2,1:T(8,128)S(1)} %get-tuple-element.197, f32[8,60,8,1]{3,0,2,1:T(8,128)S(1)} %get-tuple-element.198, f32[8,60,8,63]{3,0,2,1:T(8,128)S(1)} %get-tuple-element.199, ...), kind=kOutput, calls=%fused_computation.clone.1 | convolution fusion | flops 27525120 | bytes 5913864 | tf_op jit(solution)/shard_map/while/body/eval_jaxpr/gf,flsc->glsc/dot_general | solution.py:46
  165.1 4.4 %add_select_fusion.2 = f32[8,60,8,64]{3,0,2,1:T(8,128)S(1)} fusion(f32[8,60,8,64]{3,0,2,1:T(8,128)S(1)} %copy.145, f32[8,60,8,63]{3,0,2,1:T(8,128)S(1)} %get-tuple-element.196, f32[8,60,8,1]{3,0,2,1:T(8,128)S(1)} %get-tuple-element.197, f32[8,60,8,1]{3,0,2,1:T(8,128)S(1)} %get-tuple-element.198, f32[8,60,8,63]{3,0,2,1:T(8,128)S(1)} %get-tuple-element.199, ...), kind=kOutput, calls=%fused_computation.clone.1 | convolution fusion | flops 27525120 | bytes 5913864 | tf_op jit(solution)/shard_map/while/body/eval_jaxpr/gf,flsc->glsc/dot_general | solution.py:46
  171.7 4.4 %add_select_fusion.2 = f32[8,60,8,64]{3,0,2,1:T(8,128)S(1)} fusion(f32[8,60,8,64]{3,0,2,1:T(8,128)S(1)} %copy.145, f32[8,60,8,63]{3,0,2,1:T(8,128)S(1)} %get-tuple-element.196, f32[8,60,8,1]{3,0,2,1:T(8,128)S(1)} %get-tuple-element.197, f32[8,60,8,1]{3,0,2,1:T(8,128)S(1)} %get-tuple-element.198, f32[8,60,8,63]{3,0,2,1:T(8,128)S(1)} %get-tuple-element.199, ...), kind=kOutput, calls=%fused_computation.clone.1 | convolution fusion | flops 27525120 | bytes 5913864 | tf_op jit(solution)/shard_map/while/body/eval_jaxpr/gf,flsc->glsc/dot_general | solution.py:46
  178.4 4.4 %add_select_fusion.2 = f32[8,60,8,64]{3,0,2,1:T(8,128)S(1)} fusion(f32[8,60,8,64]{3,0,2,1:T(8,128)S(1)} %copy.145, f32[8,60,8,63]{3,0,2,1:T(8,128)S(1)} %get-tuple-element.196, f32[8,60,8,1]{3,0,2,1:T(8,128)S(1)} %get-tuple-element.197, f32[8,60,8,1]{3,0,2,1:T(8,128)S(1)} %get-tuple-element.198, f32[8,60,8,63]{3,0,2,1:T(8,128)S(1)} %get-tuple-element.199, ...), kind=kOutput, calls=%fused_computation.clone.1 | convolution fusion | flops 27525120 | bytes 5913864 | tf_op jit(solution)/shard_map/while/body/eval_jaxpr/gf,flsc->glsc/dot_general | solution.py:46
  182.8 2.1 %subtract_reduce_fusion = f32[8,60,8]{0,2,1:T(8,128)S(1)} fusion(f32[8,60,8,64]{3,0,2,1:T(8,128)S(1)} %get-tuple-element.96, f32[8,60,8,64]{3,0,2,1:T(8,128)} %bitcast.65), kind=kLoop, calls=%fused_computation.14 | loop fusion | flops 487680 | bytes 1981440 | tf_op jit(solution)/shard_map/reduce_sum | solution.py:93
  186.0 3.7 %all-to-all-start.2 = ((f32[4,1,960]{2,1,0:T(1,128)}), f32[4,1,960]{2,1,0:T(1,128)S(1)}, u32[]{:S(2)}, u32[]{:S(2)}) async-start(f32[4,1,960]{2,1,0:T(1,128)} %reshape.69), calls=%async_computation.2 | async-start | bytes 32768 | tf_op jit(solution)/shard_map/all_to_all | solution.py:94
  189.7 1.7 copy.112
  191.4 2.6 %reshape.56 = f32[8,60,512]{2,0,1:T(8,128)} reshape(f32[8,60,8,64]{3,2,0,1:T(8,128)} %copy.112) | data formatting | bytes 1966080 | tf_op jit(solution)/shard_map/reshape | solution.py:98
  194.1 8.2 %all-to-all-done.2 = f32[4,1,960]{2,1,0:T(1,128)S(1)} async-done(((f32[4,1,960]{2,1,0:T(1,128)}), f32[4,1,960]{2,1,0:T(1,128)S(1)}, u32[]{:S(2)}, u32[]{:S(2)}) %all-to-all-start.2) | async-done | bytes 15392 | tf_op jit(solution)/shard_map/all_to_all | solution.py:94
  (108 shorter events, 33.5 us)
Async XLA Ops:
  1.6 3.4 %collective-permute-start = (f32[8,15,2,4]{1,2,3,0:T(2,128)S(1)}, f32[8,15,2,4]{1,2,3,0:T(2,128)S(1)}, u32[]{:S(2)}, u32[]{:S(2)}) collective-permute-start(f32[8,15,2,4]{1,2,3,0:T(2,128)S(1)} %get-tuple-element.155), channel_id=1, source_target_pairs={{0,128},{128,256},{256,384},{384,512},{512,640},{640,768},{768,896... | collective-permute-start | bytes 11528 | tf_op jit(solution)/shard_map/ppermute | solution.py:20
  1.6 13.9 %collective-permute-start.1 = (f32[8,15,2,4]{1,2,3,0:T(2,128)S(1)}, f32[8,15,2,4]{1,2,3,0:T(2,128)S(1)}, u32[]{:S(2)}, u32[]{:S(2)}) collective-permute-start(f32[8,15,2,4]{1,2,3,0:T(2,128)S(1)} %get-tuple-element.156), channel_id=1, source_target_pairs={{128,0},{256,128},{384,256},{512,384},{640,512},{768,640},{896,768... | collective-permute-start | bytes 11528 | tf_op jit(solution)/shard_map/ppermute | solution.py:22
  15.6 10.8 %collective-permute-start.2 = (f32[8,15,12,2]{1,2,3,0:T(8,128)S(1)}, f32[8,15,12,2]{1,2,3,0:T(8,128)S(1)}, u32[]{:S(2)}, u32[]{:S(2)}) collective-permute-start(f32[8,15,12,2]{1,2,3,0:T(8,128)S(1)} %get-tuple-element.151), channel_id=1, source_target_pairs={{0,4},{4,8},{8,12},{12,16},{16,20},{20,24},{24,28},{28,32},{32,36}... | collective-permute-start | bytes 34568 | tf_op jit(solution)/shard_map/ppermute | solution.py:20
  17.6 10.3 %collective-permute-start.3 = (f32[8,15,12,2]{1,2,3,0:T(8,128)S(1)}, f32[8,15,12,2]{1,2,3,0:T(8,128)S(1)}, u32[]{:S(2)}, u32[]{:S(2)}) collective-permute-start(f32[8,15,12,2]{1,2,3,0:T(8,128)S(1)} %get-tuple-element.152), channel_id=1, source_target_pairs={{4,0},{8,4},{12,8},{16,12},{20,16},{24,20},{28,24},{32,28},{36,32}... | collective-permute-start | bytes 34568 | tf_op jit(solution)/shard_map/ppermute | solution.py:22
  28.0 16.1 %copy-start.4 = (s32[8,4]{0,1:T(4,128)S(1)}, s32[8,4]{0,1:T(4,128)}, u32[]{:S(2)}) copy-start(s32[8,4]{0,1:T(4,128)} %param.11) | copy-start | bytes 388
  28.0 16.2 %copy-start.1 = (f32[8,15,8,256]{3,2,1,0:T(8,128)S(1)}, f32[8,15,8,256]{3,2,1,0:T(8,128)}, u32[]{:S(2)}) copy-start(f32[8,15,8,256]{3,2,1,0:T(8,128)} %param.8) | copy-start | bytes 2949124
  28.5 3.6 %collective-permute-start.4 = (f32[8,15,2,4]{1,2,3,0:T(2,128)S(1)}, f32[8,15,2,4]{1,2,3,0:T(2,128)S(1)}, u32[]{:S(2)}, u32[]{:S(2)}) collective-permute-start(f32[8,15,2,4]{1,2,3,0:T(2,128)S(1)} %get-tuple-element.153), channel_id=1, source_target_pairs={{0,128},{128,256},{256,384},{384,512},{512,640},{640,768},{768,896... | collective-permute-start | bytes 11528 | tf_op jit(solution)/shard_map/ppermute | solution.py:20
  31.3 1.8 collective-permute-start.5
  33.8 11.4 %collective-permute-start.6 = (f32[8,15,12,2]{1,2,3,0:T(8,128)}, f32[8,15,12,2]{1,2,3,0:T(8,128)S(1)}, u32[]{:S(2)}, u32[]{:S(2)}) collective-permute-start(f32[8,15,12,2]{1,2,3,0:T(8,128)} %get-tuple-element.149), channel_id=1, source_target_pairs={{0,4},{4,8},{8,12},{12,16},{16,20},{20,24},{24,28},{28,32},{32,36}... | collective-permute-start | bytes 34568 | tf_op jit(solution)/shard_map/ppermute | solution.py:20
  35.8 10.8 %collective-permute-start.7 = (f32[8,15,12,2]{1,2,3,0:T(8,128)S(1)}, f32[8,15,12,2]{1,2,3,0:T(8,128)S(1)}, u32[]{:S(2)}, u32[]{:S(2)}) collective-permute-start(f32[8,15,12,2]{1,2,3,0:T(8,128)S(1)} %get-tuple-element.150), channel_id=1, source_target_pairs={{4,0},{8,4},{12,8},{16,12},{20,16},{24,20},{28,24},{32,28},{36,32}... | collective-permute-start | bytes 34568 | tf_op jit(solution)/shard_map/ppermute | solution.py:22
  44.5 2.5 %copy-start.2 = (f32[8,15,8,4]{1,3,2,0:T(4,128)S(1)}, f32[8,15,8,4]{1,3,2,0:T(4,128)}, u32[]{:S(2)}) copy-start(f32[8,15,8,4]{1,3,2,0:T(4,128)} %param.7) | copy-start | bytes 46084
  48.4 20.4 %all-to-all-start.1 = ((f32[4,1,960]{2,1,0:T(1,128)}), f32[4,1,960]{2,1,0:T(1,128)S(1)}, u32[]{:S(2)}, u32[]{:S(2)}) async-start(f32[4,1,960]{2,1,0:T(1,128)} %reshape.67), calls=%async_computation.1 | async-start | bytes 32768 | tf_op jit(solution)/shard_map/all_to_all | solution.py:86
  58.5 14.3 %copy-start.5 = (s32[8,4]{0,1:T(4,128)S(1)}, s32[8,4]{0,1:T(4,128)}, u32[]{:S(2)}) copy-start(s32[8,4]{0,1:T(4,128)} %param.10) | copy-start | bytes 388
  68.8 54.9 %all-to-all-start = ((f32[4,1,61440]{2,1,0:T(1,128)}), f32[4,1,61440]{2,1,0:T(1,128)S(1)}, u32[]{:S(2)}, u32[]{:S(2)}) async-start(f32[4,1,61440]{2,1,0:T(1,128)} %reshape.65), calls=%async_computation | async-start | bytes 1966080 | tf_op jit(solution)/shard_map/all_to_all | solution.py:85
  128.5 1.3 copy-start
  128.5 1.3 copy-start.3
  186.0 16.3 %all-to-all-start.2 = ((f32[4,1,960]{2,1,0:T(1,128)}), f32[4,1,960]{2,1,0:T(1,128)S(1)}, u32[]{:S(2)}, u32[]{:S(2)}) async-start(f32[4,1,960]{2,1,0:T(1,128)} %reshape.69), calls=%async_computation.2 | async-start | bytes 32768 | tf_op jit(solution)/shard_map/all_to_all | solution.py:94
where the time goes:
time: 205 us; the launch traced here: 204 us
  waiting for transfers between devices  83.3 us (41%)
  starting transfers between devices  39.9 us (19%)
  matrix products  37 us (18%)
  local copies, waits for them, and re-layouts  34.2 us (17%)
  other arithmetic  8.49 us (4%)
    all_to_all x1, waiting for transfers between devices, on_device(): lax.all_to_all(slotted, 'ha', split_axis=2, concat_axis=1, tiled=True)  48.6 us
    dot_general x8, matrix products, crm_update(): jnp.einsum('gf,flsc->glsc', mixing, jnp.tanh(state), precision=HIGH)  35.1 us
    ppermute x4, starting transfers between devices, extended(): lax.ppermute(head, axis, [((i + 1) % count, i) for i in range(count)])  17.8 us
    ppermute x4, waiting for transfers between devices, extended(): lax.ppermute(head, axis, [((i + 1) % count, i) for i in range(count)])  14.4 us
    slice x16, local copies, waits for them, and re-layouts, crm_update(): jnp.roll(state, -1, axis=3)  12.2 us
    all_to_all x1, waiting for transfers between devices, on_device(): lax.all_to_all(tendency, 'ha', split_axis=1, concat_axis=2, tiled=True)  8.21 us
    unnamed x22, local copies, waits for them, and re-layouts  8.09 us
    all_to_all x1, waiting for transfers between devices, on_device(): lax.all_to_all(pushes, 'ha', split_axis=2, concat_axis=1, tiled=True)  7.95 us
  transfers between devices with their start and end apart: 11, of which 11 were waited for; matrix products, arithmetic and copies ran while one was open for 6% of the time, Pallas kernels for 0%

commit v1 on v0

v1 whole, which is shorter than its diff:
```python
import jax
import jax.numpy as jnp
from jax import lax
from jax.experimental import pallas as pl
from jax.experimental.pallas import tpu as pltpu
from jax.sharding import PartitionSpec as P

MAXSUB = 8
GSUB = 4
HIGH = lax.Precision.HIGHEST
FIELDS = 8
PART = 15
ROWS = FIELDS * PART
PITCH = 16
LANES = 128
WIDTH = 64
TX = 8
TY = 4
COLS = TX * TY
HELP = 4
SLOTS = 8
PAIRS = SLOTS // 2
LEVELS = PART * HELP
BASE = 8
SROWS = 80
BLOCKS = 8

VM = pltpu.CompilerParams(vmem_limit_bytes=32 * 1024 * 1024)


def smem():
    return pl.BlockSpec(memory_space=pltpu.SMEM)


def vmem():
    return pl.BlockSpec(memory_space=pltpu.VMEM)


def slotting_kernel(assign_ref, crm_ref, out_ref, inverse, held, sems):
    loads = [
        pltpu.make_async_copy(crm_ref.at[:, i * LANES : (i + 1) * LANES], held.at[i], sems.at[i]) for i in range(TY // 2)
    ]
    for load in loads:
        load.start()
    for x in range(TX):
        for y in range(TY):
            inverse[assign_ref[y, x]] = x * TY + y
    lane = lax.broadcasted_iota(jnp.int32, (ROWS, LANES), 1)

    def column(slot, half):
        place = inverse[slot]
        x = place // TY
        y = place % TY
        rows = held[y // 2, pl.ds(x, ROWS, stride=TX), :]
        return pltpu.roll(rows, ((y % 2) ^ half) * WIDTH, 1)

    for load in loads:
        load.wait()
    for helper in range(HELP):
        for pair in range(PAIRS):
            slot = helper * SLOTS + 2 * pair
            out_ref[helper, pair * ROWS : (pair + 1) * ROWS, :] = jnp.where(
                lane < WIDTH, column(slot, 0), column(slot + 1, 1)
            )


def forcing_kernel(assign_ref, own_ref, south_ref, north_ref, west_ref, east_ref, g4_ref, f0_ref, f1_ref, f2_ref, f3_ref, ext, cols):
    me = lax.axis_index("ha")
    ext[:, 0:4, :] = west_ref[...]
    ext[0:4, 4:12, :] = south_ref[...]
    ext[4:8, 4:12, :] = own_ref[...]
    ext[8:12, 4:12, :] = north_ref[...]
    ext[:, 12:16, :] = east_ref[...]
    g = ext[...]
    for _ in range(GSUB):
        center = g[1:-1]
        east = jnp.stack([pltpu.roll(center[i], 15, 0) for i in range(center.shape[0])])
        west = jnp.stack([pltpu.roll(center[i], 1, 0) for i in range(center.shape[0])])
        north = g[2:]
        south = g[:-2]
        step = 0.2 * (east + west + north + south - 4.0 * center) - 0.15 * (east - west) - 0.15 * (north - south)
        g = center + 0.5 * step
    for y in range(TY):
        last = pltpu.roll(g[y], 12, 0)[:TX]
        g4_ref[y] = last
        cols[y] = (last - own_ref[y]) / (0.5 * GSUB)
    parts = (f0_ref, f1_ref, f2_ref, f3_ref)
    for x in range(TX):
        for y in range(TY):
            slot = assign_ref[y, x]
            away = (slot // SLOTS - me) & (HELP - 1)
            row = slot & (SLOTS - 1)
            for k in range(HELP):

                @pl.when(away == k)
                def _():
                    parts[k][pl.ds(row, 1), :] = cols[y, x : x + 1, :]


def advance_kernel(
    assign_ref, sub_ref, mix_ref, r_ref, f0_ref, f1_ref, f2_ref, f3_ref, out_ref, tend_ref, counts, one, two, push, gather, weights
):
    pair = pl.program_id(0)
    me = lax.axis_index("ha")

    @pl.when(pair == 0)
    def _():
        for x in range(TX):
            for y in range(TY):
                counts[assign_ref[y, x]] = sub_ref[y, x]
        tend_ref[...] = jnp.zeros_like(tend_ref)
        gather[...] = jnp.zeros_like(gather)
        for h in range(FIELDS):
            for g in range(FIELDS):
                weights[h, g] = jnp.full((8, LANES), 0.1 * mix_ref[h, g], jnp.float32)

    first = me * SLOTS + 2 * pair
    n0 = counts[first]
    n1 = counts[first + 1]
    lane8 = lax.broadcasted_iota(jnp.int32, (8, LANES), 1)
    limit = jnp.where(lane8 < WIDTH, n0, n1)
    steps = jnp.maximum(n0, n1)

    slot_row = lax.broadcasted_iota(jnp.int32, (SLOTS, LANES), 0)
    slot_lane = lax.broadcasted_iota(jnp.int32, (SLOTS, LANES), 1)
    chosen = slot_row == 2 * pair + slot_lane // WIDTH
    spread = jnp.where(chosen, 0.1, 0.0).astype(jnp.float32)
    averaging = jnp.where(chosen, 1.0 / WIDTH, 0.0).astype(jnp.float32)
    parts = (f0_ref, f1_ref, f2_ref, f3_ref)
    for away in range(HELP):
        start = ((me - away) & (HELP - 1)) * PART
        wide = lax.dot_general(
            parts[away][...], spread, (((0,), (0,)), ((), ())), precision=HIGH, preferred_element_type=jnp.float32
        )
        for f in range(FIELDS):
            push[f, pl.ds(start, PART), :] = wide[f * PITCH : f * PITCH + PART]

    def ends(ref):
        for f in range(FIELDS):
            ref[f, BASE - 1 : BASE, :] = ref[f, BASE : BASE + 1, :]
            ref[f, BASE + LEVELS : BASE + LEVELS + 1, :] = ref[f, BASE + LEVELS - 1 : BASE + LEVELS, :]

    for k in range(HELP):
        for f in range(FIELDS):
            one[f, BASE + k * PART : BASE + (k + 1) * PART, :] = r_ref[k, f * PART : (f + 1) * PART, :]
    ends(one)

    inner = lane8 & (WIDTH - 1)
    last = inner == WIDTH - 1
    zeroth = inner == 0

    def substep(source, target, index):
        active = index < limit
        for b in range(BLOCKS):
            row = BASE + 8 * b
            here = [source[f, row : row + 8, :] for f in range(FIELDS)]
            warm = [jnp.tanh(s) for s in here]
            for h in range(FIELDS):
                s = here[h]
                other = pltpu.roll(s, WIDTH, 1)
                right = pltpu.roll(jnp.where(zeroth, other, s), LANES - 1, 1)
                left = pltpu.roll(jnp.where(last, other, s), 1, 1)
                upper = source[h, row - 1 : row + 7, :]
                lower = source[h, row + 1 : row + 9, :]
                mixed = weights[h, 0] * warm[0]
                for g in range(1, FIELDS):
                    mixed = mixed + weights[h, g] * warm[g]
                total = 0.7 * s + push[h, 8 * b : 8 * b + 8, :]
                total = total + 0.1 * (right + left) + 0.05 * (upper + lower)
                target[h, row : row + 8, :] = jnp.where(active, total + mixed, s)
        ends(target)

    def both(index, _):
        substep(one, two, 2 * index)
        substep(two, one, 2 * index + 1)
        return 0

    lax.fori_loop(0, (steps + 1) // 2, both, 0)

    for f in range(FIELDS):
        for b in range(BLOCKS):
            n = min(8, LEVELS - 8 * b)
            out_ref[pl.ds(8 * b * FIELDS + f, n, stride=FIELDS), :] = one[f, BASE + 8 * b : BASE + 8 * b + n, :]
    for k in range(HELP):
        for f in range(FIELDS):
            gather[f * PITCH : f * PITCH + PART, :] = (
                one[f, BASE + k * PART : BASE + (k + 1) * PART, :] - r_ref[k, f * PART : (f + 1) * PART, :]
            )
        tend_ref[k] += lax.dot_general(
            averaging, gather[...], (((1,), (1,)), ((), ())), precision=HIGH, preferred_element_type=jnp.float32
        )


def placing_kernel(assign_ref, g4_ref, tend_ref, out_ref):
    for x in range(TX):
        for y in range(TY):
            out_ref[y, x : x + 1, :] = g4_ref[y, x : x + 1, :] + tend_ref[pl.ds(assign_ref[y, x], 1), :]


def shifted(count, by):
    return [(i, (i + by) % count) for i in range(count)]


def on_device(global_state, crm_state, mixing, substeps, assignment):
    f32 = jnp.float32
    assignment = assignment.T
    substeps = substeps.T
    own = jnp.pad(global_state, ((0, 0), (0, PITCH - PART), (0, 0), (0, 0)))
    own = own.transpose(3, 2, 0, 1).reshape(TY, TX, LANES)
    ny = lax.axis_size("gy")
    nx = lax.axis_size("gx")
    south = lax.ppermute(own, "gy", shifted(ny, 1))
    north = lax.ppermute(own, "gy", shifted(ny, -1))

    slotted = pl.pallas_call(
        slotting_kernel,
        out_shape=jax.ShapeDtypeStruct((HELP, PAIRS * ROWS, LANES), f32),
        in_specs=[smem(), pl.BlockSpec(memory_space=pl.ANY)],
        out_specs=vmem(),
        scratch_shapes=[
            pltpu.SMEM((COLS,), jnp.int32),
            pltpu.VMEM((TY // 2, ROWS * TX, LANES), f32),
            pltpu.SemaphoreType.DMA((TY // 2,)),
        ],
        compiler_params=VM,
    )(assignment, crm_state.reshape(ROWS * TX, TY * WIDTH))
    slotted, south, north = lax.optimization_barrier((slotted, south, north))
    arrived = lax.all_to_all(slotted, "ha", split_axis=0, concat_axis=0, tiled=True)

    tall = jnp.concatenate([south, own, north], axis=0)
    west = lax.ppermute(tall[:, TX - 4 :], "gx", shifted(nx, 1))
    east = lax.ppermute(tall[:, :4], "gx", shifted(nx, -1))
    rowshape = jax.ShapeDtypeStruct((SLOTS, LANES), f32)
    g4, f0, f1, f2, f3 = pl.pallas_call(
        forcing_kernel,
        out_shape=[jax.ShapeDtypeStruct((TY, TX, LANES), f32)] + [rowshape] * HELP,
        in_specs=[smem()] + [vmem()] * 5,
        out_specs=[vmem()] * 5,
        scratch_shapes=[pltpu.VMEM((12, 16, LANES), f32), pltpu.VMEM((TY, TX, LANES), f32)],
        compiler_params=VM,
    )(assignment, own, south, north, west, east)
    pushes = [f0] + [
        lax.ppermute(part, "ha", shifted(HELP, away)) for away, part in ((1, f1), (2, f2), (3, f3))
    ]

    whole = pl.BlockSpec((SLOTS, LANES), lambda p: (0, 0))
    final, tendency = pl.pallas_call(
        advance_kernel,
        grid=(PAIRS,),
        out_shape=[
            jax.ShapeDtypeStruct((LEVELS * FIELDS, SLOTS * WIDTH), f32),
            jax.ShapeDtypeStruct((HELP, SLOTS, LANES), f32),
        ],
        in_specs=[smem(), smem(), smem(), pl.BlockSpec((HELP, ROWS, LANES), lambda p: (0, p, 0))] + [whole] * HELP,
        out_specs=[
            pl.BlockSpec((LEVELS * FIELDS, LANES), lambda p: (0, p)),
            pl.BlockSpec((HELP, SLOTS, LANES), lambda p: (0, 0, 0)),
        ],
        scratch_shapes=[
            pltpu.SMEM((COLS,), jnp.int32),
            pltpu.VMEM((FIELDS, SROWS, LANES), f32),
            pltpu.VMEM((FIELDS, SROWS, LANES), f32),
            pltpu.VMEM((FIELDS, 64, LANES), f32),
            pltpu.VMEM((FIELDS * PITCH, LANES), f32),
            pltpu.VMEM((FIELDS, FIELDS, 8, LANES), f32),
        ],
        compiler_params=VM,
    )(assignment, substeps, mixing, arrived, *pushes)
    returned = lax.all_to_all(tendency, "ha", split_axis=0, concat_axis=0, tiled=True)
    placed = pl.pallas_call(
        placing_kernel,
        out_shape=jax.ShapeDtypeStruct((TY, TX, LANES), f32),
        in_specs=[smem(), vmem(), vmem()],
        out_specs=vmem(),
        compiler_params=VM,
    )(assignment, g4, returned.reshape(COLS, LANES))
    new_global = placed.reshape(TY, TX, FIELDS, PITCH)[..., :PART].transpose(2, 3, 1, 0)
    new_crm = final.reshape(LEVELS, FIELDS, SLOTS * WIDTH).transpose(1, 0, 2)
    return new_global, new_crm


def solution(mesh):
    in_specs = (
        P(None, "ha", "gx", "gy"),
        P(None, "ha", "gx", "gy"),
        P(),
        P("gx", "gy"),
        P("gx", "gy"),
    )
    out_specs = (P(None, "ha", "gx", "gy"), P(None, None, ("gx", "gy", "ha")))
    return jax.shard_map(
        on_device, mesh=mesh, in_specs=in_specs, out_specs=out_specs, check_vma=False
    )
```

time: 205 us -> 182 us (0.89)
  the two profiles are of different devices: /device:TPU:6 before, /device:TPU:28 now
where the time goes in v1:
time: 182 us
  Pallas kernels  85.4 us (47%)
  starting transfers between devices  49.5 us (27%)
  waiting for transfers between devices  27.9 us (15%)
  blocking collectives  14.9 us (8%)
  local copies, waits for them, and re-layouts  3.18 us (2%)
    pallas_call x1, Pallas kernels, on_device(): pl.pallas_call(advance_kernel, grid=(PAIRS,), out_shape=[jax.ShapeDtypeSt...  80.8 us
    ppermute x3, waiting for transfers between devices, on_device(): lax.ppermute(part, 'ha', shifted(HELP, away))  25 us
    ppermute x3, starting transfers between devices, on_device(): lax.ppermute(part, 'ha', shifted(HELP, away))  22.4 us
    all_to_all x1, starting transfers between devices, on_device(): lax.all_to_all(slotted, 'ha', split_axis=0, concat_axis=0, tiled=True)  18.7 us
    all_to_all x1, blocking collectives, on_device(): lax.all_to_all(tendency, 'ha', split_axis=0, concat_axis=0, tiled=True)  14.9 us
    ppermute x1, starting transfers between devices, on_device(): south = lax.ppermute(own, 'gy', shifted(ny, 1))  4.7 us
  transfers between devices with their start and end apart: 8, of which 3 were waited for; matrix products, arithmetic and copies ran while one was open for 0% of the time, Pallas kernels for 2%

profile of v1, /device:TPU:28, one launch (start us, length us, event | category | flops | bytes accessed | tf_op | source)
XLA Modules:
  0.0 181.6 jit_solution(17731914238861217215)
XLA Ops:
  0.6 0.9 pad_bitcast_fusion
  1.6 0.1 copy.7
  1.7 0.1 reshape.19.own_ref
  1.8 0.0 copy-start.1
  1.8 4.7 %collective-permute-start = (f32[4,8,128]{2,1,0:T(8,128)S(1)}, f32[4,8,128]{2,1,0:T(8,128)S(1)}, u32[]{:S(2)}, u32[]{:S(2)}) collective-permute-start(f32[4,8,128]{2,1,0:T(8,128)S(1)} %reshape.19.own_ref), channel_id=1, source_target_pairs={{0,4},{4,8},{8,12},{12,16},{16,20},{20,24},{24,28},{28,32},{32,36}... | collective-permute-start | bytes 49160 | tf_op jit(solution)/shard_map/ppermute | solution.py:212
  6.5 1.9 %collective-permute-start.1 = (f32[4,8,128]{2,1,0:T(8,128)S(1)}, f32[4,8,128]{2,1,0:T(8,128)S(1)}, u32[]{:S(2)}, u32[]{:S(2)}) collective-permute-start(f32[4,8,128]{2,1,0:T(8,128)S(1)} %reshape.19.own_ref), channel_id=1, source_target_pairs={{0,124},{4,0},{8,4},{12,8},{16,12},{20,16},{24,20},{28,24},{32,28}... | collective-permute-start | bytes 49160 | tf_op jit(solution)/shard_map/ppermute | solution.py:213
  8.4 0.0 copy-done.1
  8.4 0.0 copy-start
  8.4 1.2 copy-done
  9.6 2.4 %shard_map.68 = f32[4,480,128]{2,1,0:T(8,128)} custom-call(s32[4,8]{1,0:T(4,128)S(1)} %bitcast.17, f32[960,256]{1,0:T(8,128)S(1)} %bitcast.15), custom_call_target="tpu_custom_call" | custom-call | tf_op jit(solution)/shard_map/pallas_call | solution.py:215
  12.0 0.0 collective-permute-done.south_ref
  12.0 1.3 collective-permute-done.1.north_ref
  13.3 18.7 %all-to-all-start = ((f32[4,480,128]{2,1,0:T(8,128)}), f32[4,480,128]{2,1,0:T(8,128)S(1)}, u32[]{:S(2)}, u32[]{:S(2)}) async-start(f32[4,480,128]{2,1,0:T(8,128)} %shard_map.68), calls=%async_computation | async-start | bytes 1966080 | tf_op jit(solution)/shard_map/all_to_all | solution.py:228
  32.1 0.0 collective-permute-start.2
  32.1 1.7 collective-permute-start.3
  33.8 1.5 collective-permute-done.2.west_ref
  35.3 0.0 collective-permute-done.3.east_ref
  35.3 1.6 shard_map.69
  37.0 0.0 copy-start.2
  37.0 7.8 %collective-permute-start.4 = (f32[8,128]{1,0:T(8,128)S(1)}, f32[8,128]{1,0:T(8,128)S(1)}, u32[]{:S(2)}, u32[]{:S(2)}) collective-permute-start(f32[8,128]{1,0:T(8,128)S(1)} %get-tuple-element.17), channel_id=1, source_target_pairs={{0,1},{1,2},{2,3},{3,0},{4,5},{5,6},{6,7},{7,4},{8,9},{9,10},{10,1... | collective-permute-start | bytes 12296 | tf_op jit(solution)/shard_map/ppermute | solution.py:243
  44.8 7.3 %collective-permute-start.5 = (f32[8,128]{1,0:T(8,128)S(1)}, f32[8,128]{1,0:T(8,128)S(1)}, u32[]{:S(2)}, u32[]{:S(2)}) collective-permute-start(f32[8,128]{1,0:T(8,128)S(1)} %get-tuple-element.18), channel_id=1, source_target_pairs={{0,2},{1,3},{2,0},{3,1},{4,6},{5,7},{6,4},{7,5},{8,10},{9,11},{10,... | collective-permute-start | bytes 12296 | tf_op jit(solution)/shard_map/ppermute | solution.py:243
  52.1 0.0 copy-start.3
  52.1 7.3 %collective-permute-start.6 = (f32[8,128]{1,0:T(8,128)S(1)}, f32[8,128]{1,0:T(8,128)S(1)}, u32[]{:S(2)}, u32[]{:S(2)}) collective-permute-start(f32[8,128]{1,0:T(8,128)S(1)} %get-tuple-element.19), channel_id=1, source_target_pairs={{0,3},{1,0},{2,1},{3,2},{4,7},{5,4},{6,5},{7,6},{8,11},{9,8},{10,9... | collective-permute-start | bytes 12296 | tf_op jit(solution)/shard_map/ppermute | solution.py:243
  59.4 0.0 collective-permute-done.4.f1_ref
  59.4 25.0 %collective-permute-done.5.f2_ref = f32[8,128]{1,0:T(8,128)S(1)} collective-permute-done((f32[8,128]{1,0:T(8,128)S(1)}, f32[8,128]{1,0:T(8,128)S(1)}, u32[]{:S(2)}, u32[]{:S(2)}) %collective-permute-start.5) | collective-permute-done | bytes 4128 | tf_op jit(solution)/shard_map/ppermute | solution.py:243
  84.4 0.0 collective-permute-done.6.f3_ref
  84.4 0.0 all-to-all-done.r_ref
  84.5 80.8 %shard_map.70 = (f32[480,512]{1,0:T(8,128)}, f32[4,8,128]{2,1,0:T(8,128)S(1)}) custom-call(s32[4,8]{1,0:T(4,128)S(1)} %bitcast.19, s32[4,8]{1,0:T(4,128)S(1)} %bitcast.21, f32[8,8]{1,0:T(8,128)S(1)} %copy-done.2, f32[4,480,128]{2,1,0:T(8,128)S(1)} %all-to-all-done.r_ref, f32[8,128]{1,0:T(8,128)S(1)} %get-tuple-element.16.f0_ref, ...), custom_call_target="tpu_custom_call" | custom-call | tf_op jit(solution)/shard_map/pallas_call | solution.py:247
  165.3 14.9 %all_to_all.10 = f32[4,8,128]{2,1,0:T(8,128)S(1)} all-to-all(f32[4,8,128]{2,1,0:T(8,128)S(1)} %get-tuple-element.20), channel_id=1, replica_groups=mesh['gx'=8,'gy'=32,'ha'=4] {'ha'}, dimensions={0} | all-to-all | bytes 32768 | tf_op jit(solution)/shard_map/all_to_all | solution.py:269
  180.2 0.6 shard_map.71
  180.8 0.1 reshape.22
  180.9 0.7 copy.11
  (6 shorter events, 0.0 us)
Async XLA Ops:
  1.8 6.6 %copy-start.1 = (s32[8,4]{0,1:T(4,128)S(1)}, s32[8,4]{0,1:T(4,128)}, u32[]{:S(2)}) copy-start(s32[8,4]{0,1:T(4,128)} %param.9) | copy-start | bytes 388
  1.8 10.2 %collective-permute-start = (f32[4,8,128]{2,1,0:T(8,128)S(1)}, f32[4,8,128]{2,1,0:T(8,128)S(1)}, u32[]{:S(2)}, u32[]{:S(2)}) collective-permute-start(f32[4,8,128]{2,1,0:T(8,128)S(1)} %reshape.19.own_ref), channel_id=1, source_target_pairs={{0,4},{4,8},{8,12},{12,16},{16,20},{20,24},{24,28},{28,32},{32,36}... | collective-permute-start | bytes 49160 | tf_op jit(solution)/shard_map/ppermute | solution.py:212
  6.5 6.8 %collective-permute-start.1 = (f32[4,8,128]{2,1,0:T(8,128)S(1)}, f32[4,8,128]{2,1,0:T(8,128)S(1)}, u32[]{:S(2)}, u32[]{:S(2)}) collective-permute-start(f32[4,8,128]{2,1,0:T(8,128)S(1)} %reshape.19.own_ref), channel_id=1, source_target_pairs={{0,124},{4,0},{8,4},{12,8},{16,12},{20,16},{24,20},{28,24},{32,28}... | collective-permute-start | bytes 49160 | tf_op jit(solution)/shard_map/ppermute | solution.py:213
  8.4 1.2 copy-start
  13.3 71.1 %all-to-all-start = ((f32[4,480,128]{2,1,0:T(8,128)}), f32[4,480,128]{2,1,0:T(8,128)S(1)}, u32[]{:S(2)}, u32[]{:S(2)}) async-start(f32[4,480,128]{2,1,0:T(8,128)} %shard_map.68), calls=%async_computation | async-start | bytes 1966080 | tf_op jit(solution)/shard_map/all_to_all | solution.py:228
  32.1 3.3 %collective-permute-start.2 = (f32[12,4,128]{2,1,0:T(4,128)S(1)}, f32[12,4,128]{2,1,0:T(4,128)S(1)}, u32[]{:S(2)}, u32[]{:S(2)}) collective-permute-start(f32[12,4,128]{2,1,0:T(4,128)S(1)} %get-tuple-element.23), channel_id=1, source_target_pairs={{0,128},{128,256},{256,384},{384,512},{512,640},{640,768},{768,896... | collective-permute-start | bytes 73736 | tf_op jit(solution)/shard_map/ppermute | solution.py:231
  32.1 3.3 %collective-permute-start.3 = (f32[12,4,128]{2,1,0:T(4,128)S(1)}, f32[12,4,128]{2,1,0:T(4,128)S(1)}, u32[]{:S(2)}, u32[]{:S(2)}) collective-permute-start(f32[12,4,128]{2,1,0:T(4,128)S(1)} %get-tuple-element.22), channel_id=1, source_target_pairs={{0,896},{128,0},{256,128},{384,256},{512,384},{640,512},{768,640},... | collective-permute-start | bytes 73736 | tf_op jit(solution)/shard_map/ppermute | solution.py:232
  37.0 47.5 %copy-start.2 = (f32[8,8]{1,0:T(8,128)S(1)}, f32[8,8]{1,0:T(8,128)}, u32[]{:S(2)}) copy-start(f32[8,8]{1,0:T(8,128)} %mix_ref.1) | copy-start | bytes 772
  37.0 22.4 %collective-permute-start.4 = (f32[8,128]{1,0:T(8,128)S(1)}, f32[8,128]{1,0:T(8,128)S(1)}, u32[]{:S(2)}, u32[]{:S(2)}) collective-permute-start(f32[8,128]{1,0:T(8,128)S(1)} %get-tuple-element.17), channel_id=1, source_target_pairs={{0,1},{1,2},{2,3},{3,0},{4,5},{5,6},{6,7},{7,4},{8,9},{9,10},{10,1... | collective-permute-start | bytes 12296 | tf_op jit(solution)/shard_map/ppermute | solution.py:243
  44.8 39.6 %collective-permute-start.5 = (f32[8,128]{1,0:T(8,128)S(1)}, f32[8,128]{1,0:T(8,128)S(1)}, u32[]{:S(2)}, u32[]{:S(2)}) collective-permute-start(f32[8,128]{1,0:T(8,128)S(1)} %get-tuple-element.18), channel_id=1, source_target_pairs={{0,2},{1,3},{2,0},{3,1},{4,6},{5,7},{6,4},{7,5},{8,10},{9,11},{10,... | collective-permute-start | bytes 12296 | tf_op jit(solution)/shard_map/ppermute | solution.py:243
  52.1 32.3 %copy-start.3 = (s32[8,4]{0,1:T(4,128)S(1)}, s32[8,4]{0,1:T(4,128)}, u32[]{:S(2)}) copy-start(s32[8,4]{0,1:T(4,128)} %param.8) | copy-start | bytes 388
  52.1 32.3 %collective-permute-start.6 = (f32[8,128]{1,0:T(8,128)S(1)}, f32[8,128]{1,0:T(8,128)S(1)}, u32[]{:S(2)}, u32[]{:S(2)}) collective-permute-start(f32[8,128]{1,0:T(8,128)S(1)} %get-tuple-element.19), channel_id=1, source_target_pairs={{0,3},{1,0},{2,1},{3,2},{4,7},{5,4},{6,5},{7,6},{8,11},{9,8},{10,9... | collective-permute-start | bytes 12296 | tf_op jit(solution)/shard_map/ppermute | solution.py:243

commit v2 on v1

v2 whole, which is shorter than its diff:
```python
import jax
import jax.numpy as jnp
from jax import lax
from jax.experimental import pallas as pl
from jax.experimental.pallas import tpu as pltpu
from jax.sharding import PartitionSpec as P

MAXSUB = 8
GSUB = 4
FIELDS = 8
PART = 15
ROWS = FIELDS * PART
PITCH = 16
LANES = 128
WIDTH = 64
TX = 8
TY = 4
COLS = TX * TY
HELP = 4
SLOTS = 8
PAIRS = SLOTS // 2
LEVELS = PART * HELP
BASE = 8
SROWS = 80
BLOCKS = 8
PIECES = (0, PART - 8)

VM = pltpu.CompilerParams(vmem_limit_bytes=32 * 1024 * 1024)


def smem():
    return pl.BlockSpec(memory_space=pltpu.SMEM)


def vmem():
    return pl.BlockSpec(memory_space=pltpu.VMEM)


def slotting_kernel(assign_ref, crm_ref, out_ref, inverse, held, sems):
    loads = [
        pltpu.make_async_copy(crm_ref.at[:, i * LANES : (i + 1) * LANES], held.at[i], sems.at[i]) for i in range(TY // 2)
    ]
    for load in loads:
        load.start()
    for x in range(TX):
        for y in range(TY):
            inverse[assign_ref[y, x]] = x * TY + y
    lane = lax.broadcasted_iota(jnp.int32, (ROWS, LANES), 1)

    def column(slot, half):
        place = inverse[slot]
        x = place // TY
        y = place % TY
        rows = held[y // 2, pl.ds(x, ROWS, stride=TX), :]
        return pltpu.roll(rows, ((y % 2) ^ half) * WIDTH, 1)

    for load in loads:
        load.wait()
    for helper in range(HELP):
        for pair in range(PAIRS):
            slot = helper * SLOTS + 2 * pair
            out_ref[helper, pair * ROWS : (pair + 1) * ROWS, :] = jnp.where(
                lane < WIDTH, column(slot, 0), column(slot + 1, 1)
            )


def forcing_kernel(assign_ref, own_ref, south_ref, north_ref, west_ref, east_ref, g4_ref, f0_ref, f1_ref, f2_ref, f3_ref, ext, rows):
    me = lax.axis_index("ha")
    ext[:, 0:4, :] = west_ref[...]
    ext[0:4, 4:12, :] = south_ref[...]
    ext[4:8, 4:12, :] = own_ref[...]
    ext[8:12, 4:12, :] = north_ref[...]
    ext[:, 12:16, :] = east_ref[...]
    g = ext[...]
    for _ in range(GSUB):
        center = g[1:-1]
        east = jnp.stack([pltpu.roll(center[i], 15, 0) for i in range(center.shape[0])])
        west = jnp.stack([pltpu.roll(center[i], 1, 0) for i in range(center.shape[0])])
        north = g[2:]
        south = g[:-2]
        step = 0.2 * (east + west + north + south - 4.0 * center) - 0.15 * (east - west) - 0.15 * (north - south)
        g = center + 0.5 * step
    for y in range(TY):
        last = pltpu.roll(g[y], 12, 0)[:TX]
        g4_ref[y] = last
        forcing = (last - own_ref[y]) / (0.5 * GSUB)
        for x in range(TX):
            slot = assign_ref[y, x]
            rows[slot // SLOTS, pl.ds(slot & (SLOTS - 1), 1), :] = forcing[x : x + 1]
    for k, part in enumerate((f0_ref, f1_ref, f2_ref, f3_ref)):
        part[...] = rows[me ^ k]


def split(value):
    high = value.astype(jnp.bfloat16)
    rest = value - high.astype(jnp.float32)
    middle = rest.astype(jnp.bfloat16)
    low = (rest - middle.astype(jnp.float32)).astype(jnp.bfloat16)
    return high, middle, low


def advance_kernel(
    assign_ref,
    sub_ref,
    mix_ref,
    r_ref,
    f0_ref,
    f1_ref,
    f2_ref,
    f3_ref,
    out_ref,
    tend_ref,
    counts,
    one,
    two,
    push,
    gather,
    held,
    weights,
    staged,
    sems,
):
    me = lax.axis_index("ha")
    for x in range(TX):
        for y in range(TY):
            counts[assign_ref[y, x]] = sub_ref[y, x]
    tend_ref[...] = jnp.zeros_like(tend_ref)
    gather[...] = jnp.zeros_like(gather)
    for h in range(FIELDS):
        for g in range(FIELDS):
            weights[h, g] = jnp.full((8, LANES), 0.1 * mix_ref[h, g], jnp.float32)
    lane8 = lax.broadcasted_iota(jnp.int32, (8, LANES), 1)
    half = lane8 & WIDTH
    to_right = half | ((lane8 + 1) & (WIDTH - 1))
    to_left = half | ((lane8 + WIDTH - 1) & (WIDTH - 1))
    slot_row = lax.broadcasted_iota(jnp.int32, (SLOTS, LANES), 0)
    slot_pair = lax.broadcasted_iota(jnp.int32, (SLOTS, LANES), 1) // WIDTH
    forcings = (f0_ref, f1_ref, f2_ref, f3_ref)

    def ends(ref):
        for f in range(FIELDS):
            ref[f, BASE - 1 : BASE, :] = ref[f, BASE : BASE + 1, :]
            ref[f, BASE + LEVELS : BASE + LEVELS + 1, :] = ref[f, BASE + LEVELS - 1 : BASE + LEVELS, :]

    def send(pair, buffer):
        return pltpu.make_async_copy(
            staged.at[buffer], out_ref.at[:, pl.ds(pl.multiple_of(pair * LANES, LANES), LANES)], sems.at[buffer]
        )

    def one_pair(pair, buffer):
        first = me * SLOTS + 2 * pair
        n0 = counts[first]
        n1 = counts[first + 1]
        limit = jnp.where(lane8 < WIDTH, n0, n1)
        steps = jnp.maximum(n0, n1)
        chosen = slot_row == 2 * pair + slot_pair
        spread = jnp.where(chosen, 1.0, 0.0).astype(jnp.bfloat16)
        averaging = jnp.where(chosen, 1.0 / WIDTH, 0.0).astype(jnp.bfloat16)

        for k in range(HELP):
            terms = split(0.1 * forcings[k][...])
            total = None
            for term in terms:
                part = lax.dot_general(term, spread, (((0,), (0,)), ((), ())), preferred_element_type=jnp.float32)
                total = part if total is None else total + part
            held[k] = total
            start = (me ^ k) * PART
            for f in range(FIELDS):
                for i in PIECES:
                    push[f, pl.ds(start + i, 8), :] = held[k, f * PITCH + i : f * PITCH + i + 8, :]
        for k in range(HELP):
            for f in range(FIELDS):
                for i in PIECES:
                    row = BASE + k * PART + i
                    one[f, row : row + 8, :] = r_ref[k, pl.ds(pair * ROWS + f * PART + i, 8), :]
        ends(one)

        def substep(source, target, index):
            active = index < limit
            for b in range(BLOCKS):
                row = BASE + 8 * b
                here = [source[f, row : row + 8, :] for f in range(FIELDS)]
                warm = [jnp.tanh(s) for s in here]
                for h in range(FIELDS):
                    s = here[h]
                    right = jnp.take_along_axis(s, to_right, axis=1)
                    left = jnp.take_along_axis(s, to_left, axis=1)
                    upper = source[h, row - 1 : row + 7, :]
                    lower = source[h, row + 1 : row + 9, :]
                    mixed = weights[h, 0] * warm[0]
                    for g in range(1, FIELDS):
                        mixed = mixed + weights[h, g] * warm[g]
                    total = 0.7 * s + push[h, 8 * b : 8 * b + 8, :]
                    total = total + 0.1 * (right + left) + 0.05 * (upper + lower)
                    target[h, row : row + 8, :] = jnp.where(active, total + mixed, s)
            ends(target)

        def twice(index, _):
            substep(one, two, 2 * index)
            substep(two, one, 2 * index + 1)
            return 0

        lax.fori_loop(0, (steps + 1) // 2, twice, 0)

        for f in range(FIELDS):
            for b in range(BLOCKS):
                n = min(8, LEVELS - 8 * b)
                staged[buffer, pl.ds(8 * b * FIELDS + f, n, stride=FIELDS), :] = one[f, BASE + 8 * b : BASE + 8 * b + n, :]
        send(pair, buffer).start()
        for k in range(HELP):
            for f in range(FIELDS):
                for i in PIECES:
                    row = BASE + k * PART + i
                    gather[f * PITCH + i : f * PITCH + i + 8, :] = (
                        one[f, row : row + 8, :] - r_ref[k, pl.ds(pair * ROWS + f * PART + i, 8), :]
                    )
            for term in split(gather[...]):
                tend_ref[k] += lax.dot_general(
                    averaging, term, (((1,), (1,)), ((), ())), preferred_element_type=jnp.float32
                )

    def each(pair, _):
        one_pair(pair, pair)
        return 0

    lax.fori_loop(0, PAIRS, each, 0)
    for pair in range(PAIRS):
        send(pair, pair).wait()


def placing_kernel(assign_ref, g4_ref, tend_ref, out_ref):
    for x in range(TX):
        for y in range(TY):
            out_ref[y, x : x + 1, :] = g4_ref[y, x : x + 1, :] + tend_ref[pl.ds(assign_ref[y, x], 1), :]


def swaps(count, first):
    pairs = [(i, (i + 1) % count) for i in range(first, count, 2)]
    return pairs + [(b, a) for a, b in pairs]


def on_device(global_state, crm_state, mixing, substeps, assignment):
    f32 = jnp.float32
    assignment = assignment.T
    substeps = substeps.T
    own = jnp.pad(global_state, ((0, 0), (0, PITCH - PART), (0, 0), (0, 0)))
    own = own.transpose(3, 2, 0, 1).reshape(TY, TX, LANES)
    ny = lax.axis_size("gy")
    nx = lax.axis_size("gx")
    odd = lax.axis_index("gy") % 2 == 1
    outer = lax.ppermute(own, "gy", swaps(ny, 1))
    inner = lax.ppermute(own, "gy", swaps(ny, 0))

    slotted = pl.pallas_call(
        slotting_kernel,
        out_shape=jax.ShapeDtypeStruct((HELP, PAIRS * ROWS, LANES), f32),
        in_specs=[smem(), pl.BlockSpec(memory_space=pltpu.HBM)],
        out_specs=vmem(),
        scratch_shapes=[
            pltpu.SMEM((COLS,), jnp.int32),
            pltpu.VMEM((TY // 2, ROWS * TX, LANES), f32),
            pltpu.SemaphoreType.DMA((TY // 2,)),
        ],
        compiler_params=pltpu.CompilerParams(vmem_limit_bytes=60 * 1024 * 1024),
    )(assignment, crm_state.reshape(ROWS * TX, TY * WIDTH))
    slotted, outer, inner = lax.optimization_barrier((slotted, outer, inner))
    arrived = lax.all_to_all(slotted, "ha", split_axis=0, concat_axis=0, tiled=True)

    south = jnp.where(odd, inner, outer)
    north = jnp.where(odd, outer, inner)
    tall = jnp.concatenate([south, own, north], axis=0)
    odd = lax.axis_index("gx") % 2 == 1
    low, high = tall[:, :4], tall[:, TX - 4 :]
    outer = lax.ppermute(jnp.where(odd, high, low), "gx", swaps(nx, 1))
    inner = lax.ppermute(jnp.where(odd, low, high), "gx", swaps(nx, 0))
    west = jnp.where(odd, inner, outer)
    east = jnp.where(odd, outer, inner)
    rowshape = jax.ShapeDtypeStruct((SLOTS, LANES), f32)
    g4, *pushes = pl.pallas_call(
        forcing_kernel,
        out_shape=[jax.ShapeDtypeStruct((TY, TX, LANES), f32)] + [rowshape] * HELP,
        in_specs=[smem()] + [vmem()] * 5,
        out_specs=[vmem()] * 5,
        scratch_shapes=[pltpu.VMEM((12, 16, LANES), f32), pltpu.VMEM((HELP, SLOTS, LANES), f32)],
        compiler_params=VM,
    )(assignment, own, south, north, west, east)
    for k in range(1, HELP):
        pushes[k] = lax.ppermute(pushes[k], "ha", [(i, i ^ k) for i in range(HELP)])

    final, tendency = pl.pallas_call(
        advance_kernel,
        out_shape=[
            jax.ShapeDtypeStruct((LEVELS * FIELDS, SLOTS * WIDTH), f32),
            jax.ShapeDtypeStruct((HELP, SLOTS, LANES), f32),
        ],
        in_specs=[smem(), smem(), smem()] + [vmem()] * (1 + HELP),
        out_specs=[pl.BlockSpec(memory_space=pltpu.HBM), vmem()],
        scratch_shapes=[
            pltpu.SMEM((COLS,), jnp.int32),
            pltpu.VMEM((FIELDS, SROWS, LANES), f32),
            pltpu.VMEM((FIELDS, SROWS, LANES), f32),
            pltpu.VMEM((FIELDS, 64, LANES), f32),
            pltpu.VMEM((FIELDS * PITCH, LANES), f32),
            pltpu.VMEM((HELP, FIELDS * PITCH, LANES), f32),
            pltpu.VMEM((FIELDS, FIELDS, 8, LANES), f32),
            pltpu.VMEM((PAIRS, LEVELS * FIELDS, LANES), f32),
            pltpu.SemaphoreType.DMA((PAIRS,)),
        ],
        compiler_params=VM,
    )(assignment, substeps, mixing, arrived, *pushes)
    returned = lax.all_to_all(tendency, "ha", split_axis=0, concat_axis=0, tiled=True)
    placed = pl.pallas_call(
        placing_kernel,
        out_shape=jax.ShapeDtypeStruct((TY, TX, LANES), f32),
        in_specs=[smem(), vmem(), vmem()],
        out_specs=vmem(),
        compiler_params=VM,
    )(assignment, g4, returned.reshape(COLS, LANES))
    new_global = placed.reshape(TY, TX, FIELDS, PITCH)[..., :PART].transpose(2, 3, 1, 0)
    new_crm = final.reshape(LEVELS, FIELDS, SLOTS * WIDTH).transpose(1, 0, 2)
    return new_global, new_crm


def solution(mesh):
    in_specs = (
        P(None, "ha", "gx", "gy"),
        P(None, "ha", "gx", "gy"),
        P(),
        P("gx", "gy"),
        P("gx", "gy"),
    )
    out_specs = (P(None, "ha", "gx", "gy"), P(None, None, ("gx", "gy", "ha")))
    return jax.shard_map(
        on_device, mesh=mesh, in_specs=in_specs, out_specs=out_specs, check_vma=False
    )
```

time: 182 us -> 113 us (0.62)
  the two profiles are of different devices: /device:TPU:28 before, /device:TPU:6 now
where the time goes in v2:
time: 113 us; the launch traced here: 112 us
  starting transfers between devices  50.2 us (44%)
  waiting for transfers between devices  27.8 us (25%)
  Pallas kernels  15.8 us (14%)
  blocking collectives  14.9 us (13%)
  local copies, waits for them, and re-layouts  2.64 us (2%)
    ppermute x3, waiting for transfers between devices, on_device(): pushes[k] = lax.ppermute(pushes[k], 'ha', [(i, i ^ k) for i in range(HELP)])  26.8 us
    ppermute x3, starting transfers between devices, on_device(): pushes[k] = lax.ppermute(pushes[k], 'ha', [(i, i ^ k) for i in range(HELP)])  17 us
    all_to_all x1, starting transfers between devices, on_device(): lax.all_to_all(slotted, 'ha', split_axis=0, concat_axis=0, tiled=True)  16 us
    all_to_all x1, blocking collectives, on_device(): lax.all_to_all(tendency, 'ha', split_axis=0, concat_axis=0, tiled=True)  14.9 us
    pallas_call x1, Pallas kernels, on_device(): pl.pallas_call(advance_kernel, out_shape=[jax.ShapeDtypeStruct((LEVELS *...  10.9 us
    ppermute x1, starting transfers between devices, on_device(): outer = lax.ppermute(own, 'gy', swaps(ny, 1))  10.8 us
    pallas_call x1, Pallas kernels, on_device(): pl.pallas_call(slotting_kernel, out_shape=jax.ShapeDtypeStruct((HELP, PAI...  3.55 us
    ppermute x1, starting transfers between devices, on_device(): inner = lax.ppermute(jnp.where(odd, low, high), 'gx', swaps(nx, 0))  2.49 us
  transfers between devices with their start and end apart: 8, of which 5 were waited for; matrix products, arithmetic and copies ran while one was open for 0% of the time, Pallas kernels for 4%

profile of v2, /device:TPU:6, one launch (start us, length us, event | category | flops | bytes accessed | tf_op | source)
XLA Modules:
  0.0 112.2 jit_solution(4762663143691257821)
XLA Ops:
  0.6 0.9 pad_bitcast_fusion
  1.6 0.1 copy.7
  1.7 0.1 reshape.19.own_ref
  1.8 10.8 %collective-permute-start = (f32[4,8,128]{2,1,0:T(8,128)S(1)}, f32[4,8,128]{2,1,0:T(8,128)S(1)}, u32[]{:S(2)}, u32[]{:S(2)}) collective-permute-start(f32[4,8,128]{2,1,0:T(8,128)S(1)} %reshape.19.own_ref), channel_id=1, source_target_pairs={{4,8},{12,16},{20,24},{28,32},{36,40},{44,48},{52,56},{60,64},{68,... | collective-permute-start | bytes 49160 | tf_op jit(solution)/shard_map/ppermute | solution.py:251
  12.6 1.9 %collective-permute-start.1 = (f32[4,8,128]{2,1,0:T(8,128)S(1)}, f32[4,8,128]{2,1,0:T(8,128)S(1)}, u32[]{:S(2)}, u32[]{:S(2)}) collective-permute-start(f32[4,8,128]{2,1,0:T(8,128)S(1)} %reshape.19.own_ref), channel_id=1, source_target_pairs={{0,4},{8,12},{16,20},{24,28},{32,36},{40,44},{48,52},{56,60},{64,6... | collective-permute-start | bytes 49160 | tf_op jit(solution)/shard_map/ppermute | solution.py:252
  14.5 3.5 %shard_map.68 = f32[4,480,128]{2,1,0:T(8,128)} custom-call(s32[4,8]{1,0:T(4,128)} %bitcast.22, f32[960,256]{1,0:T(8,128)} %bitcast.27), custom_call_target="tpu_custom_call" | custom-call | tf_op jit(solution)/shard_map/pallas_call | solution.py:254
  18.1 0.0 collective-permute-done
  18.1 0.1 collective-permute-done.1
  18.2 16.0 %all-to-all-start = ((f32[4,480,128]{2,1,0:T(8,128)}), f32[4,480,128]{2,1,0:T(8,128)S(1)}, u32[]{:S(2)}, u32[]{:S(2)}) async-start(f32[4,480,128]{2,1,0:T(8,128)} %shard_map.68), calls=%async_computation | async-start | bytes 1966080 | tf_op jit(solution)/shard_map/all_to_all | solution.py:267
  34.3 1.9 %collective-permute-start.3 = (f32[12,4,128]{2,1,0:T(4,128)S(1)}, f32[12,4,128]{2,1,0:T(4,128)S(1)}, u32[]{:S(2)}, u32[]{:S(2)}) collective-permute-start(f32[12,4,128]{2,1,0:T(4,128)S(1)} %get-tuple-element.24), channel_id=1, source_target_pairs={{128,256},{384,512},{640,768},{896,0},{256,128},{512,384},{768,640... | collective-permute-start | bytes 73736 | tf_op jit(solution)/shard_map/ppermute | solution.py:274
  36.2 2.5 %collective-permute-start.2 = (f32[12,4,128]{2,1,0:T(4,128)S(1)}, f32[12,4,128]{2,1,0:T(4,128)S(1)}, u32[]{:S(2)}, u32[]{:S(2)}) collective-permute-start(f32[12,4,128]{2,1,0:T(4,128)S(1)} %get-tuple-element.25), channel_id=1, source_target_pairs={{0,128},{256,384},{512,640},{768,896},{128,0},{384,256},{640,512},... | collective-permute-start | bytes 73736 | tf_op jit(solution)/shard_map/ppermute | solution.py:275
  38.7 0.7 collective-permute-done.3
  39.4 0.1 collective-permute-done.2
  39.5 0.0 copy-start
  39.5 0.7 copy-done
  40.2 0.8 shard_map.69
  41.0 0.0 copy-start.1
  41.1 7.8 %collective-permute-start.4 = (f32[8,128]{1,0:T(8,128)S(1)}, f32[8,128]{1,0:T(8,128)S(1)}, u32[]{:S(2)}, u32[]{:S(2)}) collective-permute-start(f32[8,128]{1,0:T(8,128)S(1)} %get-tuple-element.17), channel_id=1, source_target_pairs={{0,1},{1,0},{2,3},{3,2},{4,5},{5,4},{6,7},{7,6},{8,9},{9,8},{10,11... | collective-permute-start | bytes 12296 | tf_op jit(solution)/shard_map/ppermute | solution.py:288
  48.9 7.3 %collective-permute-start.5 = (f32[8,128]{1,0:T(8,128)S(1)}, f32[8,128]{1,0:T(8,128)S(1)}, u32[]{:S(2)}, u32[]{:S(2)}) collective-permute-start(f32[8,128]{1,0:T(8,128)S(1)} %get-tuple-element.18), channel_id=1, source_target_pairs={{0,2},{1,3},{2,0},{3,1},{4,6},{5,7},{6,4},{7,5},{8,10},{9,11},{10,... | collective-permute-start | bytes 12296 | tf_op jit(solution)/shard_map/ppermute | solution.py:288
  56.2 0.0 copy-start.2
  56.2 1.9 %collective-permute-start.6 = (f32[8,128]{1,0:T(8,128)S(1)}, f32[8,128]{1,0:T(8,128)S(1)}, u32[]{:S(2)}, u32[]{:S(2)}) collective-permute-start(f32[8,128]{1,0:T(8,128)S(1)} %get-tuple-element.19), channel_id=1, source_target_pairs={{0,3},{1,2},{2,1},{3,0},{4,7},{5,6},{6,5},{7,4},{8,11},{9,10},{10,... | collective-permute-start | bytes 12296 | tf_op jit(solution)/shard_map/ppermute | solution.py:288
  58.1 22.9 %collective-permute-done.4.f1_ref = f32[8,128]{1,0:T(8,128)S(1)} collective-permute-done((f32[8,128]{1,0:T(8,128)S(1)}, f32[8,128]{1,0:T(8,128)S(1)}, u32[]{:S(2)}, u32[]{:S(2)}) %collective-permute-start.4) | collective-permute-done | bytes 4128 | tf_op jit(solution)/shard_map/ppermute | solution.py:288
  81.1 3.9 %collective-permute-done.5.f2_ref = f32[8,128]{1,0:T(8,128)S(1)} collective-permute-done((f32[8,128]{1,0:T(8,128)S(1)}, f32[8,128]{1,0:T(8,128)S(1)}, u32[]{:S(2)}, u32[]{:S(2)}) %collective-permute-start.5) | collective-permute-done | bytes 4128 | tf_op jit(solution)/shard_map/ppermute | solution.py:288
  85.0 0.0 collective-permute-done.6.f3_ref
  85.0 0.0 all-to-all-done.r_ref
  85.0 0.0 copy-done.1
  85.0 0.0 copy-done.2
  85.0 10.9 %shard_map.70 = (f32[480,512]{1,0:T(8,128)}, f32[4,8,128]{2,1,0:T(8,128)S(1)}) custom-call(s32[4,8]{1,0:T(4,128)S(1)} %bitcast.24, s32[4,8]{1,0:T(4,128)S(1)} %bitcast.26, f32[8,8]{1,0:T(8,128)S(1)} %copy-done.1, f32[4,480,128]{2,1,0:T(8,128)S(1)} %all-to-all-done.r_ref, f32[8,128]{1,0:T(8,128)S(1)} %get-tuple-element.16.f0_ref, ...), custom_call_target="tpu_custom_call" | custom-call | tf_op jit(solution)/shard_map/pallas_call | solution.py:290
  95.8 14.9 %all_to_all.10 = f32[4,8,128]{2,1,0:T(8,128)S(1)} all-to-all(f32[4,8,128]{2,1,0:T(8,128)S(1)} %get-tuple-element.20), channel_id=1, replica_groups=mesh['gx'=8,'gy'=32,'ha'=4] {'ha'}, dimensions={0} | all-to-all | bytes 32768 | tf_op jit(solution)/shard_map/all_to_all | solution.py:311
  110.8 0.6 shard_map.71
  111.4 0.1 reshape.22
  111.5 0.7 copy.11
  (4 shorter events, 0.0 us)
Async XLA Ops:
  1.8 16.3 %collective-permute-start = (f32[4,8,128]{2,1,0:T(8,128)S(1)}, f32[4,8,128]{2,1,0:T(8,128)S(1)}, u32[]{:S(2)}, u32[]{:S(2)}) collective-permute-start(f32[4,8,128]{2,1,0:T(8,128)S(1)} %reshape.19.own_ref), channel_id=1, source_target_pairs={{4,8},{12,16},{20,24},{28,32},{36,40},{44,48},{52,56},{60,64},{68,... | collective-permute-start | bytes 49160 | tf_op jit(solution)/shard_map/ppermute | solution.py:251
  12.6 5.6 %collective-permute-start.1 = (f32[4,8,128]{2,1,0:T(8,128)S(1)}, f32[4,8,128]{2,1,0:T(8,128)S(1)}, u32[]{:S(2)}, u32[]{:S(2)}) collective-permute-start(f32[4,8,128]{2,1,0:T(8,128)S(1)} %reshape.19.own_ref), channel_id=1, source_target_pairs={{0,4},{8,12},{16,20},{24,28},{32,36},{40,44},{48,52},{56,60},{64,6... | collective-permute-start | bytes 49160 | tf_op jit(solution)/shard_map/ppermute | solution.py:252
  18.2 66.8 %all-to-all-start = ((f32[4,480,128]{2,1,0:T(8,128)}), f32[4,480,128]{2,1,0:T(8,128)S(1)}, u32[]{:S(2)}, u32[]{:S(2)}) async-start(f32[4,480,128]{2,1,0:T(8,128)} %shard_map.68), calls=%async_computation | async-start | bytes 1966080 | tf_op jit(solution)/shard_map/all_to_all | solution.py:267
  34.3 5.1 %collective-permute-start.3 = (f32[12,4,128]{2,1,0:T(4,128)S(1)}, f32[12,4,128]{2,1,0:T(4,128)S(1)}, u32[]{:S(2)}, u32[]{:S(2)}) collective-permute-start(f32[12,4,128]{2,1,0:T(4,128)S(1)} %get-tuple-element.24), channel_id=1, source_target_pairs={{128,256},{384,512},{640,768},{896,0},{256,128},{512,384},{768,640... | collective-permute-start | bytes 73736 | tf_op jit(solution)/shard_map/ppermute | solution.py:274
  36.2 3.3 %collective-permute-start.2 = (f32[12,4,128]{2,1,0:T(4,128)S(1)}, f32[12,4,128]{2,1,0:T(4,128)S(1)}, u32[]{:S(2)}, u32[]{:S(2)}) collective-permute-start(f32[12,4,128]{2,1,0:T(4,128)S(1)} %get-tuple-element.25), channel_id=1, source_target_pairs={{0,128},{256,384},{512,640},{768,896},{128,0},{384,256},{640,512},... | collective-permute-start | bytes 73736 | tf_op jit(solution)/shard_map/ppermute | solution.py:275
  39.5 0.7 copy-start
  41.0 43.9 %copy-start.1 = (f32[8,8]{1,0:T(8,128)S(1)}, f32[8,8]{1,0:T(8,128)}, u32[]{:S(2)}) copy-start(f32[8,8]{1,0:T(8,128)} %mix_ref.1) | copy-start | bytes 772
  41.1 40.0 %collective-permute-start.4 = (f32[8,128]{1,0:T(8,128)S(1)}, f32[8,128]{1,0:T(8,128)S(1)}, u32[]{:S(2)}, u32[]{:S(2)}) collective-permute-start(f32[8,128]{1,0:T(8,128)S(1)} %get-tuple-element.17), channel_id=1, source_target_pairs={{0,1},{1,0},{2,3},{3,2},{4,5},{5,4},{6,7},{7,6},{8,9},{9,8},{10,11... | collective-permute-start | bytes 12296 | tf_op jit(solution)/shard_map/ppermute | solution.py:288
  48.9 36.1 %collective-permute-start.5 = (f32[8,128]{1,0:T(8,128)S(1)}, f32[8,128]{1,0:T(8,128)S(1)}, u32[]{:S(2)}, u32[]{:S(2)}) collective-permute-start(f32[8,128]{1,0:T(8,128)S(1)} %get-tuple-element.18), channel_id=1, source_target_pairs={{0,2},{1,3},{2,0},{3,1},{4,6},{5,7},{6,4},{7,5},{8,10},{9,11},{10,... | collective-permute-start | bytes 12296 | tf_op jit(solution)/shard_map/ppermute | solution.py:288
  56.2 28.8 %copy-start.2 = (s32[8,4]{0,1:T(4,128)S(1)}, s32[8,4]{0,1:T(4,128)}, u32[]{:S(2)}) copy-start(s32[8,4]{0,1:T(4,128)} %param.8) | copy-start | bytes 388
  56.2 28.8 %collective-permute-start.6 = (f32[8,128]{1,0:T(8,128)S(1)}, f32[8,128]{1,0:T(8,128)S(1)}, u32[]{:S(2)}, u32[]{:S(2)}) collective-permute-start(f32[8,128]{1,0:T(8,128)S(1)} %get-tuple-element.19), channel_id=1, source_target_pairs={{0,3},{1,2},{2,1},{3,0},{4,7},{5,6},{6,5},{7,4},{8,11},{9,10},{10,... | collective-permute-start | bytes 12296 | tf_op jit(solution)/shard_map/ppermute | solution.py:288

commit v3 on v2

--- a/solution.py
+++ b/solution.py
@@ -17,6 +17,7 @@
 TY = 4
 COLS = TX * TY
 HELP = 4
+ORDER = (0, 1, 3, 2)
 SLOTS = 8
 PAIRS = SLOTS // 2
 LEVELS = PART * HELP
@@ -36,7 +37,8 @@
     return pl.BlockSpec(memory_space=pltpu.VMEM)
 
 
-def slotting_kernel(assign_ref, crm_ref, out_ref, inverse, held, sems):
+def slotting_kernel(assign_ref, crm_ref, s0_ref, s1_ref, s2_ref, s3_ref, inverse, held, sems):
+    me = lax.axis_index("ha")
     loads = [
         pltpu.make_async_copy(crm_ref.at[:, i * LANES : (i + 1) * LANES], held.at[i], sems.at[i]) for i in range(TY // 2)
     ]
@@ -56,21 +58,36 @@
 
     for load in loads:
         load.wait()
-    for helper in range(HELP):
+    for k, part in enumerate((s0_ref, s1_ref, s2_ref, s3_ref)):
         for pair in range(PAIRS):
-            slot = helper * SLOTS + 2 * pair
-            out_ref[helper, pair * ROWS : (pair + 1) * ROWS, :] = jnp.where(
-                lane < WIDTH, column(slot, 0), column(slot + 1, 1)
-            )
-
-
-def forcing_kernel(assign_ref, own_ref, south_ref, north_ref, west_ref, east_ref, g4_ref, f0_ref, f1_ref, f2_ref, f3_ref, ext, rows):
+            slot = (me ^ ORDER[k]) * SLOTS + 2 * pair
+            part[pair * ROWS : (pair + 1) * ROWS, :] = jnp.where(lane < WIDTH, column(slot, 0), column(slot + 1, 1))
+
+
+def choose(odd, first, second):
+    return jnp.where(odd, first, second)
+
+
+def border_kernel(own_ref, outer_ref, inner_ref, to_outer_ref, to_inner_ref, tall):
+    odd = lax.axis_index("gy") % 2 == 1
+    tall[0:4] = choose(odd, inner_ref[...], outer_ref[...])
+    tall[4:8] = own_ref[...]
+    tall[8:12] = choose(odd, outer_ref[...], inner_ref[...])
+    odd = lax.axis_index("gx") % 2 == 1
+    low, high = tall[:, 0:4, :], tall[:, TX - 4 : TX, :]
+    to_outer_ref[...] = choose(odd, high, low)
+    to_inner_ref[...] = choose(odd, low, high)
+
+
+def forcing_kernel(assign_ref, own_ref, outery_ref, innery_ref, outerx_ref, innerx_ref, g4_ref, f0_ref, f1_ref, f2_ref, f3_ref, ext, rows):
     me = lax.axis_index("ha")
-    ext[:, 0:4, :] = west_ref[...]
-    ext[0:4, 4:12, :] = south_ref[...]
+    odd = lax.axis_index("gy") % 2 == 1
+    ext[0:4, 4:12, :] = choose(odd, innery_ref[...], outery_ref[...])
     ext[4:8, 4:12, :] = own_ref[...]
-    ext[8:12, 4:12, :] = north_ref[...]
-    ext[:, 12:16, :] = east_ref[...]
+    ext[8:12, 4:12, :] = choose(odd, outery_ref[...], innery_ref[...])
+    odd = lax.axis_index("gx") % 2 == 1
+    ext[:, 0:4, :] = choose(odd, innerx_ref[...], outerx_ref[...])
+    ext[:, 12:16, :] = choose(odd, outerx_ref[...], innerx_ref[...])
     g = ext[...]
     for _ in range(GSUB):
         center = g[1:-1]
@@ -88,7 +105,7 @@
             slot = assign_ref[y, x]
             rows[slot // SLOTS, pl.ds(slot & (SLOTS - 1), 1), :] = forcing[x : x + 1]
     for k, part in enumerate((f0_ref, f1_ref, f2_ref, f3_ref)):
-        part[...] = rows[me ^ k]
+        part[...] = rows[me ^ ORDER[k]]
 
 
 def split(value):
@@ -103,7 +120,10 @@
     assign_ref,
     sub_ref,
     mix_ref,
-    r_ref,
+    r0_ref,
+    r1_ref,
+    r2_ref,
+    r3_ref,
     f0_ref,
     f1_ref,
     f2_ref,
@@ -135,6 +155,7 @@
     to_left = half | ((lane8 + WIDTH - 1) & (WIDTH - 1))
     slot_row = lax.broadcasted_iota(jnp.int32, (SLOTS, LANES), 0)
     slot_pair = lax.broadcasted_iota(jnp.int32, (SLOTS, LANES), 1) // WIDTH
+    arrived = (r0_ref, r1_ref, r2_ref, r3_ref)
     forcings = (f0_ref, f1_ref, f2_ref, f3_ref)
 
     def ends(ref):
@@ -164,15 +185,13 @@
                 part = lax.dot_general(term, spread, (((0,), (0,)), ((), ())), preferred_element_type=jnp.float32)
                 total = part if total is None else total + part
             held[k] = total
-            start = (me ^ k) * PART
+            start = (me ^ ORDER[k]) * PART
             for f in range(FIELDS):
                 for i in PIECES:
                     push[f, pl.ds(start + i, 8), :] = held[k, f * PITCH + i : f * PITCH + i + 8, :]
-        for k in range(HELP):
             for f in range(FIELDS):
                 for i in PIECES:
-                    row = BASE + k * PART + i
-                    one[f, row : row + 8, :] = r_ref[k, pl.ds(pair * ROWS + f * PART + i, 8), :]
+                    one[f, pl.ds(BASE + start + i, 8), :] = arrived[k][pl.ds(pair * ROWS + f * PART + i, 8), :]
         ends(one)
 
         def substep(source, target, index):
@@ -200,7 +219,13 @@
             substep(two, one, 2 * index + 1)
             return 0
 
-        lax.fori_loop(0, (steps + 1) // 2, twice, 0)
+        lax.fori_loop(0, steps // 2, twice, 0)
+
+        @pl.when(steps % 2 == 1)
+        def _():
+            substep(one, two, steps - 1)
+            for f in range(FIELDS):
+                one[f, BASE : BASE + 64, :] = two[f, BASE : BASE + 64, :]
 
         for f in range(FIELDS):
             for b in range(BLOCKS):
@@ -208,16 +233,17 @@
                 staged[buffer, pl.ds(8 * b * FIELDS + f, n, stride=FIELDS), :] = one[f, BASE + 8 * b : BASE + 8 * b + n, :]
         send(pair, buffer).start()
         for k in range(HELP):
+            owner = me ^ ORDER[k]
             for f in range(FIELDS):
                 for i in PIECES:
-                    row = BASE + k * PART + i
                     gather[f * PITCH + i : f * PITCH + i + 8, :] = (
-                        one[f, row : row + 8, :] - r_ref[k, pl.ds(pair * ROWS + f * PART + i, 8), :]
+                        one[f, pl.ds(BASE + owner * PART + i, 8), :] - arrived[k][pl.ds(pair * ROWS + f * PART + i, 8), :]
                     )
+            total = None
             for term in split(gather[...]):
-                tend_ref[k] += lax.dot_general(
-                    averaging, term, (((1,), (1,)), ((), ())), preferred_element_type=jnp.float32
-                )
+                part = lax.dot_general(averaging, term, (((1,), (1,)), ((), ())), preferred_element_type=jnp.float32)
+                total = part if total is None else total + part
+            tend_ref[owner] += total
 
     def each(pair, _):
         one_pair(pair, pair)
@@ -228,15 +254,23 @@
         send(pair, pair).wait()
 
 
-def placing_kernel(assign_ref, g4_ref, tend_ref, out_ref):
+def placing_kernel(assign_ref, g4_ref, tend_ref, out_ref, rows, turned):
     for x in range(TX):
         for y in range(TY):
-            out_ref[y, x : x + 1, :] = g4_ref[y, x : x + 1, :] + tend_ref[pl.ds(assign_ref[y, x], 1), :]
+            rows[x * TY + y : x * TY + y + 1, :] = g4_ref[y, x : x + 1, :] + tend_ref[pl.ds(assign_ref[y, x], 1), :]
+    for f in range(FIELDS):
+        turned[f] = pltpu.roll(rows[...], (LANES - f * PITCH) % LANES, 1)
+        for x in range(TX):
+            out_ref[f, x] = turned[f, x * TY : (x + 1) * TY, :PART]
 
 
 def swaps(count, first):
     pairs = [(i, (i + 1) % count) for i in range(first, count, 2)]
     return pairs + [(b, a) for a, b in pairs]
+
+
+def partners(k):
+    return [(i, i ^ k) for i in range(HELP)]
 
 
 def on_device(global_state, crm_state, mixing, substeps, assignment):
@@ -247,15 +281,14 @@
     own = own.transpose(3, 2, 0, 1).reshape(TY, TX, LANES)
     ny = lax.axis_size("gy")
     nx = lax.axis_size("gx")
-    odd = lax.axis_index("gy") % 2 == 1
     outer = lax.ppermute(own, "gy", swaps(ny, 1))
     inner = lax.ppermute(own, "gy", swaps(ny, 0))
 
     slotted = pl.pallas_call(
         slotting_kernel,
-        out_shape=jax.ShapeDtypeStruct((HELP, PAIRS * ROWS, LANES), f32),
+        out_shape=[jax.ShapeDtypeStruct((PAIRS * ROWS, LANES), f32)] * HELP,
         in_specs=[smem(), pl.BlockSpec(memory_space=pltpu.HBM)],
-        out_specs=vmem(),
+        out_specs=[vmem()] * HELP,
         scratch_shapes=[
             pltpu.SMEM((COLS,), jnp.int32),
             pltpu.VMEM((TY // 2, ROWS * TX, LANES), f32),
@@ -263,18 +296,21 @@
         ],
         compiler_params=pltpu.CompilerParams(vmem_limit_bytes=60 * 1024 * 1024),
     )(assignment, crm_state.reshape(ROWS * TX, TY * WIDTH))
-    slotted, outer, inner = lax.optimization_barrier((slotted, outer, inner))
-    arrived = lax.all_to_all(slotted, "ha", split_axis=0, concat_axis=0, tiled=True)
-
-    south = jnp.where(odd, inner, outer)
-    north = jnp.where(odd, outer, inner)
-    tall = jnp.concatenate([south, own, north], axis=0)
-    odd = lax.axis_index("gx") % 2 == 1
-    low, high = tall[:, :4], tall[:, TX - 4 :]
-    outer = lax.ppermute(jnp.where(odd, high, low), "gx", swaps(nx, 1))
-    inner = lax.ppermute(jnp.where(odd, low, high), "gx", swaps(nx, 0))
-    west = jnp.where(odd, inner, outer)
-    east = jnp.where(odd, outer, inner)
+    *slotted, outer, inner = lax.optimization_barrier((*slotted, outer, inner))
+    arrived = [slotted[0]] + [lax.ppermute(slotted[k], "ha", partners(ORDER[k])) for k in range(1, HELP)]
+
+    edge = jax.ShapeDtypeStruct((3 * TY, 4, LANES), f32)
+    to_outer, to_inner = pl.pallas_call(
+        border_kernel,
+        out_shape=[edge, edge],
+        in_specs=[vmem()] * 3,
+        out_specs=[vmem()] * 2,
+        scratch_shapes=[pltpu.VMEM((3 * TY, TX, LANES), f32)],
+        cost_estimate=pl.CostEstimate(flops=1000, bytes_accessed=300_000, transcendentals=0),
+        compiler_params=VM,
+    )(own, outer, inner)
+    outerx = lax.ppermute(to_outer, "gx", swaps(nx, 1))
+    innerx = lax.ppermute(to_inner, "gx", swaps(nx, 0))
     rowshape = jax.ShapeDtypeStruct((SLOTS, LANES), f32)
     g4, *pushes = pl.pallas_call(
         forcing_kernel,
@@ -283,9 +319,9 @@
         out_specs=[vmem()] * 5,
         scratch_shapes=[pltpu.VMEM((12, 16, LANES), f32), pltpu.VMEM((HELP, SLOTS, LANES), f32)],
         compiler_params=VM,
-    )(assignment, own, south, north, west, east)
+    )(assignment, own, outer, inner, outerx, innerx)
     for k in range(1, HELP):
-        pushes[k] = lax.ppermute(pushes[k], "ha", [(i, i ^ k) for i in range(HELP)])
+        pushes[k] = lax.ppermute(pushes[k], "ha", partners(ORDER[k]))
 
     final, tendency = pl.pallas_call(
         advance_kernel,
@@ -293,7 +329,7 @@
             jax.ShapeDtypeStruct((LEVELS * FIELDS, SLOTS * WIDTH), f32),
             jax.ShapeDtypeStruct((HELP, SLOTS, LANES), f32),
         ],
-        in_specs=[smem(), smem(), smem()] + [vmem()] * (1 + HELP),
+        in_specs=[smem(), smem(), smem()] + [vmem()] * (2 * HELP),
         out_specs=[pl.BlockSpec(memory_space=pltpu.HBM), vmem()],
         scratch_shapes=[
             pltpu.SMEM((COLS,), jnp.int32),
@@ -307,16 +343,17 @@
             pltpu.SemaphoreType.DMA((PAIRS,)),
         ],
         compiler_params=VM,
-    )(assignment, substeps, mixing, arrived, *pushes)
+    )(assignment, substeps, mixing, *arrived, *pushes)
     returned = lax.all_to_all(tendency, "ha", split_axis=0, concat_axis=0, tiled=True)
     placed = pl.pallas_call(
         placing_kernel,
-        out_shape=jax.ShapeDtypeStruct((TY, TX, LANES), f32),
+        out_shape=jax.ShapeDtypeStruct((FIELDS, TX, TY, PART), f32),
         in_specs=[smem(), vmem(), vmem()],
         out_specs=vmem(),
+        scratch_shapes=[pltpu.VMEM((COLS, LANES), f32), pltpu.VMEM((FIELDS, COLS, LANES), f32)],
         compiler_params=VM,
     )(assignment, g4, returned.reshape(COLS, LANES))
-    new_global = placed.reshape(TY, TX, FIELDS, PITCH)[..., :PART].transpose(2, 3, 1, 0)
+    new_global = placed.transpose(0, 3, 1, 2)
     new_crm = final.reshape(LEVELS, FIELDS, SLOTS * WIDTH).transpose(1, 0, 2)
     return new_global, new_crm
 

time: 113 us -> 121 us (1.071)
  the two profiles are of different devices: /device:TPU:6 before, /device:TPU:26 now
where the time goes in v3:
time: 121 us; the launch traced here: 120 us
  starting transfers between devices  54.5 us (45%)
  blocking collectives  27 us (22%)
  waiting for transfers between devices  19.3 us (16%)
  Pallas kernels  16.4 us (14%)
  local copies, waits for them, and re-layouts  2.07 us (2%)
    ppermute x3, starting transfers between devices, on_device(): lax.ppermute(slotted[k], 'ha', partners(ORDER[k]))  27.4 us
    all_to_all x1, blocking collectives, on_device(): lax.all_to_all(tendency, 'ha', split_axis=0, concat_axis=0, tiled=True)  27 us
    ppermute x3, waiting for transfers between devices, on_device(): pushes[k] = lax.ppermute(pushes[k], 'ha', partners(ORDER[k]))  18.5 us
    ppermute x3, starting transfers between devices, on_device(): pushes[k] = lax.ppermute(pushes[k], 'ha', partners(ORDER[k]))  14.4 us
    pallas_call x1, Pallas kernels, on_device(): pl.pallas_call(advance_kernel, out_shape=[jax.ShapeDtypeStruct((LEVELS *...  10.7 us
    ppermute x1, starting transfers between devices, on_device(): outer = lax.ppermute(own, 'gy', swaps(ny, 1))  4.92 us
    ppermute x1, starting transfers between devices, on_device(): innerx = lax.ppermute(to_inner, 'gx', swaps(nx, 0))  3.5 us
    pallas_call x1, Pallas kernels, on_device(): pl.pallas_call(slotting_kernel, out_shape=[jax.ShapeDtypeStruct((PAIRS *...  3.46 us
  transfers between devices with their start and end apart: 10, of which 4 were waited for; matrix products, arithmetic and copies ran while one was open for 0% of the time, Pallas kernels for 4%

profile of v3, /device:TPU:26, one launch (start us, length us, event | category | flops | bytes accessed | tf_op | source)
XLA Modules:
  0.0 120.1 jit_solution(6444560125430616956)
XLA Ops:
  0.6 0.9 pad_bitcast_fusion
  1.6 0.1 copy.7
  1.7 0.1 reshape.16.own_ref
  1.8 2.4 %collective-permute-start.1 = (f32[4,8,128]{2,1,0:T(8,128)S(1)}, f32[4,8,128]{2,1,0:T(8,128)S(1)}, u32[]{:S(2)}, u32[]{:S(2)}) collective-permute-start(f32[4,8,128]{2,1,0:T(8,128)S(1)} %reshape.16.own_ref), channel_id=1, source_target_pairs={{0,4},{8,12},{16,20},{24,28},{32,36},{40,44},{48,52},{56,60},{64,6... | collective-permute-start | bytes 49160 | tf_op jit(solution)/shard_map/ppermute | solution.py:285
  4.1 4.9 %collective-permute-start = (f32[4,8,128]{2,1,0:T(8,128)S(1)}, f32[4,8,128]{2,1,0:T(8,128)S(1)}, u32[]{:S(2)}, u32[]{:S(2)}) collective-permute-start(f32[4,8,128]{2,1,0:T(8,128)S(1)} %reshape.16.own_ref), channel_id=1, source_target_pairs={{4,8},{12,16},{20,24},{28,32},{36,40},{44,48},{52,56},{60,64},{68,... | collective-permute-start | bytes 49160 | tf_op jit(solution)/shard_map/ppermute | solution.py:284
  9.1 3.5 %shard_map.68 = (f32[480,128]{1,0:T(8,128)}, f32[480,128]{1,0:T(8,128)}, f32[480,128]{1,0:T(8,128)}, f32[480,128]{1,0:T(8,128)}) custom-call(s32[4,8]{1,0:T(4,128)} %bitcast.13, f32[960,256]{1,0:T(8,128)} %bitcast.18), custom_call_target="tpu_custom_call" | custom-call | tf_op jit(solution)/shard_map/pallas_call | solution.py:287
  12.5 0.0 collective-permute-done.1.inner_ref.innery_ref
  12.5 0.0 collective-permute-done.outer_ref.outery_ref
  12.5 10.9 %collective-permute-start.4 = (f32[480,128]{1,0:T(8,128)}, f32[480,128]{1,0:T(8,128)S(1)}, u32[]{:S(2)}, u32[]{:S(2)}) collective-permute-start(f32[480,128]{1,0:T(8,128)} %get-tuple-element.31), channel_id=1, source_target_pairs={{0,1},{1,0},{2,3},{3,2},{4,5},{5,4},{6,7},{7,6},{8,9},{9,8},{10,11... | collective-permute-start | bytes 737288 | tf_op jit(solution)/shard_map/ppermute | solution.py:300
  23.5 10.9 %collective-permute-start.5 = (f32[480,128]{1,0:T(8,128)}, f32[480,128]{1,0:T(8,128)S(1)}, u32[]{:S(2)}, u32[]{:S(2)}) collective-permute-start(f32[480,128]{1,0:T(8,128)} %get-tuple-element.32), channel_id=1, source_target_pairs={{0,3},{1,2},{2,1},{3,0},{4,7},{5,6},{6,5},{7,4},{8,11},{9,10},{10,... | collective-permute-start | bytes 737288 | tf_op jit(solution)/shard_map/ppermute | solution.py:300
  34.4 5.6 %collective-permute-start.6 = (f32[480,128]{1,0:T(8,128)}, f32[480,128]{1,0:T(8,128)S(1)}, u32[]{:S(2)}, u32[]{:S(2)}) collective-permute-start(f32[480,128]{1,0:T(8,128)} %get-tuple-element.33), channel_id=1, source_target_pairs={{0,2},{1,3},{2,0},{3,1},{4,6},{5,7},{6,4},{7,5},{8,10},{9,11},{10,... | collective-permute-start | bytes 737288 | tf_op jit(solution)/shard_map/ppermute | solution.py:300
  40.0 0.0 copy-start.1
  40.0 1.9 %collective-permute-start.2 = (f32[12,4,128]{2,1,0:T(4,128)S(1)}, f32[12,4,128]{2,1,0:T(4,128)S(1)}, u32[]{:S(2)}, u32[]{:S(2)}) collective-permute-start(f32[12,4,128]{2,1,0:T(4,128)S(1)} %get-tuple-element.27), channel_id=1, source_target_pairs={{128,256},{384,512},{640,768},{896,0},{256,128},{512,384},{768,640... | collective-permute-start | bytes 73736 | tf_op jit(solution)/shard_map/ppermute | solution.py:312
  41.9 3.5 %collective-permute-start.3 = (f32[12,4,128]{2,1,0:T(4,128)S(1)}, f32[12,4,128]{2,1,0:T(4,128)S(1)}, u32[]{:S(2)}, u32[]{:S(2)}) collective-permute-start(f32[12,4,128]{2,1,0:T(4,128)S(1)} %get-tuple-element.28), channel_id=1, source_target_pairs={{0,128},{256,384},{512,640},{768,896},{128,0},{384,256},{640,512},... | collective-permute-start | bytes 73736 | tf_op jit(solution)/shard_map/ppermute | solution.py:313
  45.5 0.0 collective-permute-done.2.outerx_ref
  45.5 0.8 collective-permute-done.3.innerx_ref
  46.3 0.8 shard_map.70
  47.1 0.0 copy-start.2
  47.1 3.6 %collective-permute-start.7 = (f32[8,128]{1,0:T(8,128)S(1)}, f32[8,128]{1,0:T(8,128)S(1)}, u32[]{:S(2)}, u32[]{:S(2)}) collective-permute-start(f32[8,128]{1,0:T(8,128)S(1)} %get-tuple-element.35), channel_id=1, source_target_pairs={{0,1},{1,0},{2,3},{3,2},{4,5},{5,4},{6,7},{7,6},{8,9},{9,8},{10,11... | collective-permute-start | bytes 12296 | tf_op jit(solution)/shard_map/ppermute | solution.py:324
  50.8 7.8 %collective-permute-start.8 = (f32[8,128]{1,0:T(8,128)S(1)}, f32[8,128]{1,0:T(8,128)S(1)}, u32[]{:S(2)}, u32[]{:S(2)}) collective-permute-start(f32[8,128]{1,0:T(8,128)S(1)} %get-tuple-element.36), channel_id=1, source_target_pairs={{0,3},{1,2},{2,1},{3,0},{4,7},{5,6},{6,5},{7,4},{8,11},{9,10},{10,... | collective-permute-start | bytes 12296 | tf_op jit(solution)/shard_map/ppermute | solution.py:324
  58.6 6.7 %collective-permute-done.7.f1_ref = f32[8,128]{1,0:T(8,128)S(1)} collective-permute-done((f32[8,128]{1,0:T(8,128)S(1)}, f32[8,128]{1,0:T(8,128)S(1)}, u32[]{:S(2)}, u32[]{:S(2)}) %collective-permute-start.7) | collective-permute-done | bytes 4128 | tf_op jit(solution)/shard_map/ppermute | solution.py:324
  65.4 2.9 %collective-permute-start.9 = (f32[8,128]{1,0:T(8,128)S(1)}, f32[8,128]{1,0:T(8,128)S(1)}, u32[]{:S(2)}, u32[]{:S(2)}) collective-permute-start(f32[8,128]{1,0:T(8,128)S(1)} %get-tuple-element.37), channel_id=1, source_target_pairs={{0,2},{1,3},{2,0},{3,1},{4,6},{5,7},{6,4},{7,5},{8,10},{9,11},{10,... | collective-permute-start | bytes 12296 | tf_op jit(solution)/shard_map/ppermute | solution.py:324
  68.3 8.2 %collective-permute-done.8.f2_ref = f32[8,128]{1,0:T(8,128)S(1)} collective-permute-done((f32[8,128]{1,0:T(8,128)S(1)}, f32[8,128]{1,0:T(8,128)S(1)}, u32[]{:S(2)}, u32[]{:S(2)}) %collective-permute-start.8) | collective-permute-done | bytes 4128 | tf_op jit(solution)/shard_map/ppermute | solution.py:324
  76.5 3.5 %collective-permute-done.9.f3_ref = f32[8,128]{1,0:T(8,128)S(1)} collective-permute-done((f32[8,128]{1,0:T(8,128)S(1)}, f32[8,128]{1,0:T(8,128)S(1)}, u32[]{:S(2)}, u32[]{:S(2)}) %collective-permute-start.9) | collective-permute-done | bytes 4128 | tf_op jit(solution)/shard_map/ppermute | solution.py:324
  80.1 0.0 collective-permute-done.4.r1_ref
  80.1 0.0 collective-permute-done.5.r2_ref
  80.1 0.0 collective-permute-done.6.r3_ref
  80.1 0.0 copy-start
  80.1 0.9 copy-done
  81.0 10.7 %shard_map.71 = (f32[480,512]{1,0:T(8,128)}, f32[4,8,128]{2,1,0:T(8,128)S(1)}) custom-call(s32[4,8]{1,0:T(4,128)S(1)} %bitcast.15, s32[4,8]{1,0:T(4,128)S(1)} %bitcast.17, f32[8,8]{1,0:T(8,128)S(1)} %copy-done.2, f32[480,128]{1,0:T(8,128)S(1)} %copy-done, f32[480,128]{1,0:T(8,128)S(1)} %collective-permute-done.4.r1_ref, ...), custom_call_target="tpu_custom_call" | custom-call | tf_op jit(solution)/shard_map/pallas_call | solution.py:326
  91.8 27.0 %all_to_all.5 = f32[4,8,128]{2,1,0:T(8,128)S(1)} all-to-all(f32[4,8,128]{2,1,0:T(8,128)S(1)} %get-tuple-element.38), channel_id=1, replica_groups=mesh['gx'=8,'gy'=32,'ha'=4] {'ha'}, dimensions={0} | all-to-all | bytes 32768 | tf_op jit(solution)/shard_map/all_to_all | solution.py:347
  118.7 1.4 %shard_map.72 = f32[8,8,4,15]{3,2,1,0:T(4,128)} custom-call(s32[4,8]{1,0:T(4,128)S(1)} %bitcast.16, f32[4,8,128]{2,1,0:T(8,128)S(1)} %get-tuple-element.29.g4_ref, f32[32,128]{1,0:T(8,128)S(1)} %bitcast.12), custom_call_target="tpu_custom_call" | custom-call | tf_op jit(solution)/shard_map/pallas_call | solution.py:348
  (5 shorter events, 0.0 us)
Async XLA Ops:
  1.8 10.8 %collective-permute-start.1 = (f32[4,8,128]{2,1,0:T(8,128)S(1)}, f32[4,8,128]{2,1,0:T(8,128)S(1)}, u32[]{:S(2)}, u32[]{:S(2)}) collective-permute-start(f32[4,8,128]{2,1,0:T(8,128)S(1)} %reshape.16.own_ref), channel_id=1, source_target_pairs={{0,4},{8,12},{16,20},{24,28},{32,36},{40,44},{48,52},{56,60},{64,6... | collective-permute-start | bytes 49160 | tf_op jit(solution)/shard_map/ppermute | solution.py:285
  4.1 8.4 %collective-permute-start = (f32[4,8,128]{2,1,0:T(8,128)S(1)}, f32[4,8,128]{2,1,0:T(8,128)S(1)}, u32[]{:S(2)}, u32[]{:S(2)}) collective-permute-start(f32[4,8,128]{2,1,0:T(8,128)S(1)} %reshape.16.own_ref), channel_id=1, source_target_pairs={{4,8},{12,16},{20,24},{28,32},{36,40},{44,48},{52,56},{60,64},{68,... | collective-permute-start | bytes 49160 | tf_op jit(solution)/shard_map/ppermute | solution.py:284
  12.5 67.5 %collective-permute-start.4 = (f32[480,128]{1,0:T(8,128)}, f32[480,128]{1,0:T(8,128)S(1)}, u32[]{:S(2)}, u32[]{:S(2)}) collective-permute-start(f32[480,128]{1,0:T(8,128)} %get-tuple-element.31), channel_id=1, source_target_pairs={{0,1},{1,0},{2,3},{3,2},{4,5},{5,4},{6,7},{7,6},{8,9},{9,8},{10,11... | collective-permute-start | bytes 737288 | tf_op jit(solution)/shard_map/ppermute | solution.py:300
  23.5 56.6 %collective-permute-start.5 = (f32[480,128]{1,0:T(8,128)}, f32[480,128]{1,0:T(8,128)S(1)}, u32[]{:S(2)}, u32[]{:S(2)}) collective-permute-start(f32[480,128]{1,0:T(8,128)} %get-tuple-element.32), channel_id=1, source_target_pairs={{0,3},{1,2},{2,1},{3,0},{4,7},{5,6},{6,5},{7,4},{8,11},{9,10},{10,... | collective-permute-start | bytes 737288 | tf_op jit(solution)/shard_map/ppermute | solution.py:300
  34.4 45.7 %collective-permute-start.6 = (f32[480,128]{1,0:T(8,128)}, f32[480,128]{1,0:T(8,128)S(1)}, u32[]{:S(2)}, u32[]{:S(2)}) collective-permute-start(f32[480,128]{1,0:T(8,128)} %get-tuple-element.33), channel_id=1, source_target_pairs={{0,2},{1,3},{2,0},{3,1},{4,6},{5,7},{6,4},{7,5},{8,10},{9,11},{10,... | collective-permute-start | bytes 737288 | tf_op jit(solution)/shard_map/ppermute | solution.py:300
  40.0 6.3 %copy-start.1 = (s32[8,4]{0,1:T(4,128)S(1)}, s32[8,4]{0,1:T(4,128)}, u32[]{:S(2)}) copy-start(s32[8,4]{0,1:T(4,128)} %param.9) | copy-start | bytes 388
  40.0 5.4 %collective-permute-start.2 = (f32[12,4,128]{2,1,0:T(4,128)S(1)}, f32[12,4,128]{2,1,0:T(4,128)S(1)}, u32[]{:S(2)}, u32[]{:S(2)}) collective-permute-start(f32[12,4,128]{2,1,0:T(4,128)S(1)} %get-tuple-element.27), channel_id=1, source_target_pairs={{128,256},{384,512},{640,768},{896,0},{256,128},{512,384},{768,640... | collective-permute-start | bytes 73736 | tf_op jit(solution)/shard_map/ppermute | solution.py:312
  41.9 4.3 %collective-permute-start.3 = (f32[12,4,128]{2,1,0:T(4,128)S(1)}, f32[12,4,128]{2,1,0:T(4,128)S(1)}, u32[]{:S(2)}, u32[]{:S(2)}) collective-permute-start(f32[12,4,128]{2,1,0:T(4,128)S(1)} %get-tuple-element.28), channel_id=1, source_target_pairs={{0,128},{256,384},{512,640},{768,896},{128,0},{384,256},{640,512},... | collective-permute-start | bytes 73736 | tf_op jit(solution)/shard_map/ppermute | solution.py:313
  47.1 32.9 %copy-start.2 = (f32[8,8]{1,0:T(8,128)S(1)}, f32[8,8]{1,0:T(8,128)}, u32[]{:S(2)}) copy-start(f32[8,8]{1,0:T(8,128)} %mix_ref.1) | copy-start | bytes 772
  47.1 18.2 %collective-permute-start.7 = (f32[8,128]{1,0:T(8,128)S(1)}, f32[8,128]{1,0:T(8,128)S(1)}, u32[]{:S(2)}, u32[]{:S(2)}) collective-permute-start(f32[8,128]{1,0:T(8,128)S(1)} %get-tuple-element.35), channel_id=1, source_target_pairs={{0,1},{1,0},{2,3},{3,2},{4,5},{5,4},{6,7},{7,6},{8,9},{9,8},{10,11... | collective-permute-start | bytes 12296 | tf_op jit(solution)/shard_map/ppermute | solution.py:324
  50.8 25.7 %collective-permute-start.8 = (f32[8,128]{1,0:T(8,128)S(1)}, f32[8,128]{1,0:T(8,128)S(1)}, u32[]{:S(2)}, u32[]{:S(2)}) collective-permute-start(f32[8,128]{1,0:T(8,128)S(1)} %get-tuple-element.36), channel_id=1, source_target_pairs={{0,3},{1,2},{2,1},{3,0},{4,7},{5,6},{6,5},{7,4},{8,11},{9,10},{10,... | collective-permute-start | bytes 12296 | tf_op jit(solution)/shard_map/ppermute | solution.py:324
  65.4 14.7 %copy-start.3 = (s32[8,4]{0,1:T(4,128)S(1)}, s32[8,4]{0,1:T(4,128)}, u32[]{:S(2)}) copy-start(s32[8,4]{0,1:T(4,128)} %param.8) | copy-start | bytes 388
  65.4 14.7 %collective-permute-start.9 = (f32[8,128]{1,0:T(8,128)S(1)}, f32[8,128]{1,0:T(8,128)S(1)}, u32[]{:S(2)}, u32[]{:S(2)}) collective-permute-start(f32[8,128]{1,0:T(8,128)S(1)} %get-tuple-element.37), channel_id=1, source_target_pairs={{0,2},{1,3},{2,0},{3,1},{4,6},{5,7},{6,4},{7,5},{8,10},{9,11},{10,... | collective-permute-start | bytes 12296 | tf_op jit(solution)/shard_map/ppermute | solution.py:324
  80.1 0.9 copy-start

commit v4 on v3

--- a/solution.py
+++ b/solution.py
@@ -79,8 +79,7 @@
     to_inner_ref[...] = choose(odd, low, high)
 
 
-def forcing_kernel(assign_ref, own_ref, outery_ref, innery_ref, outerx_ref, innerx_ref, g4_ref, f0_ref, f1_ref, f2_ref, f3_ref, ext, rows):
-    me = lax.axis_index("ha")
+def forcing_kernel(assign_ref, own_ref, outery_ref, innery_ref, outerx_ref, innerx_ref, g4_ref, rows_ref, ext):
     odd = lax.axis_index("gy") % 2 == 1
     ext[0:4, 4:12, :] = choose(odd, innery_ref[...], outery_ref[...])
     ext[4:8, 4:12, :] = own_ref[...]
@@ -103,9 +102,7 @@
         forcing = (last - own_ref[y]) / (0.5 * GSUB)
         for x in range(TX):
             slot = assign_ref[y, x]
-            rows[slot // SLOTS, pl.ds(slot & (SLOTS - 1), 1), :] = forcing[x : x + 1]
-    for k, part in enumerate((f0_ref, f1_ref, f2_ref, f3_ref)):
-        part[...] = rows[me ^ ORDER[k]]
+            rows_ref[slot // SLOTS, pl.ds(slot & (SLOTS - 1), 1), :] = forcing[x : x + 1]
 
 
 def split(value):
@@ -124,10 +121,7 @@
     r1_ref,
     r2_ref,
     r3_ref,
-    f0_ref,
-    f1_ref,
-    f2_ref,
-    f3_ref,
+    push_ref,
     out_ref,
     tend_ref,
     counts,
@@ -138,8 +132,11 @@
     held,
     weights,
     staged,
+    mine,
     sems,
 ):
+    load = pltpu.make_async_copy(r0_ref, mine, sems.at[PAIRS])
+    load.start()
     me = lax.axis_index("ha")
     for x in range(TX):
         for y in range(TY):
@@ -155,8 +152,7 @@
     to_left = half | ((lane8 + WIDTH - 1) & (WIDTH - 1))
     slot_row = lax.broadcasted_iota(jnp.int32, (SLOTS, LANES), 0)
     slot_pair = lax.broadcasted_iota(jnp.int32, (SLOTS, LANES), 1) // WIDTH
-    arrived = (r0_ref, r1_ref, r2_ref, r3_ref)
-    forcings = (f0_ref, f1_ref, f2_ref, f3_ref)
+    arrived = (mine, r1_ref, r2_ref, r3_ref)
 
     def ends(ref):
         for f in range(FIELDS):
@@ -179,7 +175,7 @@
         averaging = jnp.where(chosen, 1.0 / WIDTH, 0.0).astype(jnp.bfloat16)
 
         for k in range(HELP):
-            terms = split(0.1 * forcings[k][...])
+            terms = split(0.1 * push_ref[k])
             total = None
             for term in terms:
                 part = lax.dot_general(term, spread, (((0,), (0,)), ((), ())), preferred_element_type=jnp.float32)
@@ -188,7 +184,7 @@
             start = (me ^ ORDER[k]) * PART
             for f in range(FIELDS):
                 for i in PIECES:
-                    push[f, pl.ds(start + i, 8), :] = held[k, f * PITCH + i : f * PITCH + i + 8, :]
+                    push[f, k * PART + i : k * PART + i + 8, :] = held[k, f * PITCH + i : f * PITCH + i + 8, :]
             for f in range(FIELDS):
                 for i in PIECES:
                     one[f, pl.ds(BASE + start + i, 8), :] = arrived[k][pl.ds(pair * ROWS + f * PART + i, 8), :]
@@ -249,6 +245,7 @@
         one_pair(pair, pair)
         return 0
 
+    load.wait()
     lax.fori_loop(0, PAIRS, each, 0)
     for pair in range(PAIRS):
         send(pair, pair).wait()
@@ -296,7 +293,7 @@
         ],
         compiler_params=pltpu.CompilerParams(vmem_limit_bytes=60 * 1024 * 1024),
     )(assignment, crm_state.reshape(ROWS * TX, TY * WIDTH))
-    *slotted, outer, inner = lax.optimization_barrier((*slotted, outer, inner))
+    *slotted, outer = lax.optimization_barrier((*slotted, outer))
     arrived = [slotted[0]] + [lax.ppermute(slotted[k], "ha", partners(ORDER[k])) for k in range(1, HELP)]
 
     edge = jax.ShapeDtypeStruct((3 * TY, 4, LANES), f32)
@@ -311,17 +308,18 @@
     )(own, outer, inner)
     outerx = lax.ppermute(to_outer, "gx", swaps(nx, 1))
     innerx = lax.ppermute(to_inner, "gx", swaps(nx, 0))
-    rowshape = jax.ShapeDtypeStruct((SLOTS, LANES), f32)
-    g4, *pushes = pl.pallas_call(
+    g4, pushes = pl.pallas_call(
         forcing_kernel,
-        out_shape=[jax.ShapeDtypeStruct((TY, TX, LANES), f32)] + [rowshape] * HELP,
+        out_shape=[
+            jax.ShapeDtypeStruct((TY, TX, LANES), f32),
+            jax.ShapeDtypeStruct((HELP, SLOTS, LANES), f32),
+        ],
         in_specs=[smem()] + [vmem()] * 5,
-        out_specs=[vmem()] * 5,
-        scratch_shapes=[pltpu.VMEM((12, 16, LANES), f32), pltpu.VMEM((HELP, SLOTS, LANES), f32)],
+        out_specs=[vmem()] * 2,
+        scratch_shapes=[pltpu.VMEM((12, 16, LANES), f32)],
         compiler_params=VM,
     )(assignment, own, outer, inner, outerx, innerx)
-    for k in range(1, HELP):
-        pushes[k] = lax.ppermute(pushes[k], "ha", partners(ORDER[k]))
+    pushes = lax.all_to_all(pushes, "ha", split_axis=0, concat_axis=0, tiled=True)
 
     final, tendency = pl.pallas_call(
         advance_kernel,
@@ -329,7 +327,7 @@
             jax.ShapeDtypeStruct((LEVELS * FIELDS, SLOTS * WIDTH), f32),
             jax.ShapeDtypeStruct((HELP, SLOTS, LANES), f32),
         ],
-        in_specs=[smem(), smem(), smem()] + [vmem()] * (2 * HELP),
+        in_specs=[smem(), smem(), smem()] + [pl.BlockSpec(memory_space=pltpu.HBM)] + [vmem()] * HELP,
         out_specs=[pl.BlockSpec(memory_space=pltpu.HBM), vmem()],
         scratch_shapes=[
             pltpu.SMEM((COLS,), jnp.int32),
@@ -340,10 +338,11 @@
             pltpu.VMEM((HELP, FIELDS * PITCH, LANES), f32),
             pltpu.VMEM((FIELDS, FIELDS, 8, LANES), f32),
             pltpu.VMEM((PAIRS, LEVELS * FIELDS, LANES), f32),
-            pltpu.SemaphoreType.DMA((PAIRS,)),
+            pltpu.VMEM((PAIRS * ROWS, LANES), f32),
+            pltpu.SemaphoreType.DMA((PAIRS + 1,)),
         ],
         compiler_params=VM,
-    )(assignment, substeps, mixing, *arrived, *pushes)
+    )(assignment, substeps, mixing, *arrived, pushes)
     returned = lax.all_to_all(tendency, "ha", split_axis=0, concat_axis=0, tiled=True)
     placed = pl.pallas_call(
         placing_kernel,

time: 121 us -> 112 us (0.926)
  the two profiles are of different devices: /device:TPU:26 before, /device:TPU:6 now
where the time goes in v4:
time: 112 us
  starting transfers between devices  48.7 us (43%)
  blocking collectives  39.9 us (36%)
  Pallas kernels  15.9 us (14%)
  waiting for transfers between devices  4.53 us (4%)
  local copies, waits for them, and re-layouts  2.07 us (2%)
    all_to_all x1, blocking collectives, on_device(): lax.all_to_all(pushes, 'ha', split_axis=0, concat_axis=0, tiled=True)  24.9 us
    ppermute x3, starting transfers between devices, on_device(): lax.ppermute(slotted[k], 'ha', partners(ORDER[k]))  24.7 us
    all_to_all x1, blocking collectives, on_device(): lax.all_to_all(tendency, 'ha', split_axis=0, concat_axis=0, tiled=True)  14.9 us
    ppermute x1, starting transfers between devices, on_device(): outer = lax.ppermute(own, 'gy', swaps(ny, 1))  10.8 us
    pallas_call x1, Pallas kernels, on_device(): pl.pallas_call(advance_kernel, out_shape=[jax.ShapeDtypeStruct((LEVELS *...  10.3 us
    ppermute x1, starting transfers between devices, on_device(): innerx = lax.ppermute(to_inner, 'gx', swaps(nx, 0))  9.4 us
    ppermute x1, waiting for transfers between devices, on_device(): inner = lax.ppermute(own, 'gy', swaps(ny, 0))  3.7 us
    pallas_call x1, Pallas kernels, on_device(): pl.pallas_call(slotting_kernel, out_shape=[jax.ShapeDtypeStruct((PAIRS *...  3.44 us
  transfers between devices with their start and end apart: 7, of which 2 were waited for; matrix products, arithmetic and copies ran while one was open for 0% of the time, Pallas kernels for 4%

profile of v4, /device:TPU:6, one launch (start us, length us, event | category | flops | bytes accessed | tf_op | source)
XLA Modules:
  0.0 112.0 jit_solution(2399639939138366111)
XLA Ops:
  0.6 0.9 pad_bitcast_fusion
  1.6 0.1 copy.7
  1.7 0.1 reshape.16.own_ref
  1.8 10.8 %collective-permute-start = (f32[4,8,128]{2,1,0:T(8,128)S(1)}, f32[4,8,128]{2,1,0:T(8,128)S(1)}, u32[]{:S(2)}, u32[]{:S(2)}) collective-permute-start(f32[4,8,128]{2,1,0:T(8,128)S(1)} %reshape.16.own_ref), channel_id=1, source_target_pairs={{4,8},{12,16},{20,24},{28,32},{36,40},{44,48},{52,56},{60,64},{68,... | collective-permute-start | bytes 49160 | tf_op jit(solution)/shard_map/ppermute | solution.py:281
  12.6 3.4 %shard_map.68 = (f32[480,128]{1,0:T(8,128)}, f32[480,128]{1,0:T(8,128)}, f32[480,128]{1,0:T(8,128)}, f32[480,128]{1,0:T(8,128)}) custom-call(s32[4,8]{1,0:T(4,128)} %bitcast.13, f32[960,256]{1,0:T(8,128)} %bitcast.18), custom_call_target="tpu_custom_call" | custom-call | tf_op jit(solution)/shard_map/pallas_call | solution.py:284
  16.0 0.0 collective-permute-done.outer_ref.outery_ref
  16.0 10.9 %collective-permute-start.4 = (f32[480,128]{1,0:T(8,128)}, f32[480,128]{1,0:T(8,128)S(1)}, u32[]{:S(2)}, u32[]{:S(2)}) collective-permute-start(f32[480,128]{1,0:T(8,128)} %get-tuple-element.26), channel_id=1, source_target_pairs={{0,1},{1,0},{2,3},{3,2},{4,5},{5,4},{6,7},{7,6},{8,9},{9,8},{10,11... | collective-permute-start | bytes 737288 | tf_op jit(solution)/shard_map/ppermute | solution.py:297
  27.0 8.2 %collective-permute-start.5 = (f32[480,128]{1,0:T(8,128)}, f32[480,128]{1,0:T(8,128)S(1)}, u32[]{:S(2)}, u32[]{:S(2)}) collective-permute-start(f32[480,128]{1,0:T(8,128)} %get-tuple-element.27), channel_id=1, source_target_pairs={{0,3},{1,2},{2,1},{3,0},{4,7},{5,6},{6,5},{7,4},{8,11},{9,10},{10,... | collective-permute-start | bytes 737288 | tf_op jit(solution)/shard_map/ppermute | solution.py:297
  35.2 5.6 %collective-permute-start.6 = (f32[480,128]{1,0:T(8,128)}, f32[480,128]{1,0:T(8,128)S(1)}, u32[]{:S(2)}, u32[]{:S(2)}) collective-permute-start(f32[480,128]{1,0:T(8,128)} %get-tuple-element.28), channel_id=1, source_target_pairs={{0,2},{1,3},{2,0},{3,1},{4,6},{5,7},{6,4},{7,5},{8,10},{9,11},{10,... | collective-permute-start | bytes 737288 | tf_op jit(solution)/shard_map/ppermute | solution.py:297
  40.7 1.9 %collective-permute-start.1 = (f32[4,8,128]{2,1,0:T(8,128)S(1)}, f32[4,8,128]{2,1,0:T(8,128)S(1)}, u32[]{:S(2)}, u32[]{:S(2)}) collective-permute-start(f32[4,8,128]{2,1,0:T(8,128)S(1)} %reshape.16.own_ref), channel_id=1, source_target_pairs={{0,4},{8,12},{16,20},{24,28},{32,36},{40,44},{48,52},{56,60},{64,6... | collective-permute-start | bytes 49160 | tf_op jit(solution)/shard_map/ppermute | solution.py:282
  42.7 3.7 %collective-permute-done.1.inner_ref.innery_ref = f32[4,8,128]{2,1,0:T(8,128)S(1)} collective-permute-done((f32[4,8,128]{2,1,0:T(8,128)S(1)}, f32[4,8,128]{2,1,0:T(8,128)S(1)}, u32[]{:S(2)}, u32[]{:S(2)}) %collective-permute-start.1) | collective-permute-done | bytes 16416 | tf_op jit(solution)/shard_map/ppermute | solution.py:282
  46.4 0.0 copy-start.1
  46.4 1.9 %collective-permute-start.2 = (f32[12,4,128]{2,1,0:T(4,128)S(1)}, f32[12,4,128]{2,1,0:T(4,128)S(1)}, u32[]{:S(2)}, u32[]{:S(2)}) collective-permute-start(f32[12,4,128]{2,1,0:T(4,128)S(1)} %get-tuple-element.22), channel_id=1, source_target_pairs={{128,256},{384,512},{640,768},{896,0},{256,128},{512,384},{768,640... | collective-permute-start | bytes 73736 | tf_op jit(solution)/shard_map/ppermute | solution.py:309
  48.3 9.4 %collective-permute-start.3 = (f32[12,4,128]{2,1,0:T(4,128)S(1)}, f32[12,4,128]{2,1,0:T(4,128)S(1)}, u32[]{:S(2)}, u32[]{:S(2)}) collective-permute-start(f32[12,4,128]{2,1,0:T(4,128)S(1)} %get-tuple-element.23), channel_id=1, source_target_pairs={{0,128},{256,384},{512,640},{768,896},{128,0},{384,256},{640,512},... | collective-permute-start | bytes 73736 | tf_op jit(solution)/shard_map/ppermute | solution.py:310
  57.8 0.0 collective-permute-done.2.outerx_ref
  57.8 0.8 collective-permute-done.3.innerx_ref
  58.6 0.0 copy-done.1
  58.6 0.8 shard_map.70
  59.4 0.0 copy-start.2
  59.5 0.0 copy-start.3
  59.5 24.9 %all_to_all.10.push_ref = f32[4,8,128]{2,1,0:T(8,128)S(1)} all-to-all(f32[4,8,128]{2,1,0:T(8,128)S(1)} %get-tuple-element.29), channel_id=1, replica_groups=mesh['gx'=8,'gy'=32,'ha'=4] {'ha'}, dimensions={0} | all-to-all | bytes 32768 | tf_op jit(solution)/shard_map/all_to_all | solution.py:322
  84.4 0.0 collective-permute-done.4.r1_ref
  84.4 0.0 collective-permute-done.5.r2_ref
  84.4 0.0 collective-permute-done.6.r3_ref
  84.4 0.0 copy-done.2
  84.4 0.0 copy-done.3
  84.4 0.0 copy-start
  84.5 0.9 copy-done
  85.4 10.3 %shard_map.71 = (f32[480,512]{1,0:T(8,128)}, f32[4,8,128]{2,1,0:T(8,128)S(1)}) custom-call(s32[4,8]{1,0:T(4,128)S(1)} %bitcast.15, s32[4,8]{1,0:T(4,128)S(1)} %bitcast.17, f32[8,8]{1,0:T(8,128)S(1)} %copy-done.2, f32[480,128]{1,0:T(8,128)S(1)} %copy-done, f32[480,128]{1,0:T(8,128)S(1)} %collective-permute-done.4.r1_ref, ...), custom_call_target="tpu_custom_call" | custom-call | tf_op jit(solution)/shard_map/pallas_call | solution.py:324
  95.7 14.9 %all_to_all.11 = f32[4,8,128]{2,1,0:T(8,128)S(1)} all-to-all(f32[4,8,128]{2,1,0:T(8,128)S(1)} %get-tuple-element.30), channel_id=1, replica_groups=mesh['gx'=8,'gy'=32,'ha'=4] {'ha'}, dimensions={0} | all-to-all | bytes 32768 | tf_op jit(solution)/shard_map/all_to_all | solution.py:346
  110.6 1.4 %shard_map.72 = f32[8,8,4,15]{3,2,1,0:T(4,128)} custom-call(s32[4,8]{1,0:T(4,128)S(1)} %bitcast.16, f32[4,8,128]{2,1,0:T(8,128)S(1)} %get-tuple-element.24.g4_ref, f32[32,128]{1,0:T(8,128)S(1)} %bitcast.12), custom_call_target="tpu_custom_call" | custom-call | tf_op jit(solution)/shard_map/pallas_call | solution.py:347
  (1 shorter events, 0.0 us)
Async XLA Ops:
  1.8 14.3 %collective-permute-start = (f32[4,8,128]{2,1,0:T(8,128)S(1)}, f32[4,8,128]{2,1,0:T(8,128)S(1)}, u32[]{:S(2)}, u32[]{:S(2)}) collective-permute-start(f32[4,8,128]{2,1,0:T(8,128)S(1)} %reshape.16.own_ref), channel_id=1, source_target_pairs={{4,8},{12,16},{20,24},{28,32},{36,40},{44,48},{52,56},{60,64},{68,... | collective-permute-start | bytes 49160 | tf_op jit(solution)/shard_map/ppermute | solution.py:281
  16.0 68.4 %collective-permute-start.4 = (f32[480,128]{1,0:T(8,128)}, f32[480,128]{1,0:T(8,128)S(1)}, u32[]{:S(2)}, u32[]{:S(2)}) collective-permute-start(f32[480,128]{1,0:T(8,128)} %get-tuple-element.26), channel_id=1, source_target_pairs={{0,1},{1,0},{2,3},{3,2},{4,5},{5,4},{6,7},{7,6},{8,9},{9,8},{10,11... | collective-permute-start | bytes 737288 | tf_op jit(solution)/shard_map/ppermute | solution.py:297
  27.0 57.5 %collective-permute-start.5 = (f32[480,128]{1,0:T(8,128)}, f32[480,128]{1,0:T(8,128)S(1)}, u32[]{:S(2)}, u32[]{:S(2)}) collective-permute-start(f32[480,128]{1,0:T(8,128)} %get-tuple-element.27), channel_id=1, source_target_pairs={{0,3},{1,2},{2,1},{3,0},{4,7},{5,6},{6,5},{7,4},{8,11},{9,10},{10,... | collective-permute-start | bytes 737288 | tf_op jit(solution)/shard_map/ppermute | solution.py:297
  35.2 49.2 %collective-permute-start.6 = (f32[480,128]{1,0:T(8,128)}, f32[480,128]{1,0:T(8,128)S(1)}, u32[]{:S(2)}, u32[]{:S(2)}) collective-permute-start(f32[480,128]{1,0:T(8,128)} %get-tuple-element.28), channel_id=1, source_target_pairs={{0,2},{1,3},{2,0},{3,1},{4,6},{5,7},{6,4},{7,5},{8,10},{9,11},{10,... | collective-permute-start | bytes 737288 | tf_op jit(solution)/shard_map/ppermute | solution.py:297
  40.7 5.6 %collective-permute-start.1 = (f32[4,8,128]{2,1,0:T(8,128)S(1)}, f32[4,8,128]{2,1,0:T(8,128)S(1)}, u32[]{:S(2)}, u32[]{:S(2)}) collective-permute-start(f32[4,8,128]{2,1,0:T(8,128)S(1)} %reshape.16.own_ref), channel_id=1, source_target_pairs={{0,4},{8,12},{16,20},{24,28},{32,36},{40,44},{48,52},{56,60},{64,6... | collective-permute-start | bytes 49160 | tf_op jit(solution)/shard_map/ppermute | solution.py:282
  46.4 12.2 %copy-start.1 = (s32[8,4]{0,1:T(4,128)S(1)}, s32[8,4]{0,1:T(4,128)}, u32[]{:S(2)}) copy-start(s32[8,4]{0,1:T(4,128)} %param.9) | copy-start | bytes 388
  46.4 11.3 %collective-permute-start.2 = (f32[12,4,128]{2,1,0:T(4,128)S(1)}, f32[12,4,128]{2,1,0:T(4,128)S(1)}, u32[]{:S(2)}, u32[]{:S(2)}) collective-permute-start(f32[12,4,128]{2,1,0:T(4,128)S(1)} %get-tuple-element.22), channel_id=1, source_target_pairs={{128,256},{384,512},{640,768},{896,0},{256,128},{512,384},{768,640... | collective-permute-start | bytes 73736 | tf_op jit(solution)/shard_map/ppermute | solution.py:309
  48.3 10.2 %collective-permute-start.3 = (f32[12,4,128]{2,1,0:T(4,128)S(1)}, f32[12,4,128]{2,1,0:T(4,128)S(1)}, u32[]{:S(2)}, u32[]{:S(2)}) collective-permute-start(f32[12,4,128]{2,1,0:T(4,128)S(1)} %get-tuple-element.23), channel_id=1, source_target_pairs={{0,128},{256,384},{512,640},{768,896},{128,0},{384,256},{640,512},... | collective-permute-start | bytes 73736 | tf_op jit(solution)/shard_map/ppermute | solution.py:310
  59.4 25.0 %copy-start.2 = (f32[8,8]{1,0:T(8,128)S(1)}, f32[8,8]{1,0:T(8,128)}, u32[]{:S(2)}) copy-start(f32[8,8]{1,0:T(8,128)} %mix_ref.1) | copy-start | bytes 772
  59.5 25.0 %copy-start.3 = (s32[8,4]{0,1:T(4,128)S(1)}, s32[8,4]{0,1:T(4,128)}, u32[]{:S(2)}) copy-start(s32[8,4]{0,1:T(4,128)} %param.8) | copy-start | bytes 388
  84.4 0.9 copy-start

commit v5 on v4

--- a/solution.py
+++ b/solution.py
@@ -17,7 +17,7 @@
 TY = 4
 COLS = TX * TY
 HELP = 4
-ORDER = (0, 1, 3, 2)
+ORDER = (0, 2, 1, 3)
 SLOTS = 8
 PAIRS = SLOTS // 2
 LEVELS = PART * HELP
@@ -79,7 +79,9 @@
     to_inner_ref[...] = choose(odd, low, high)
 
 
-def forcing_kernel(assign_ref, own_ref, outery_ref, innery_ref, outerx_ref, innerx_ref, g4_ref, rows_ref, ext):
+def forcing_kernel(assign_ref, own_ref, outery_ref, innery_ref, outerx_ref, innerx_ref, s0_ref, g4_ref, rows_ref, mine_ref, ext, sem):
+    load = pltpu.make_async_copy(s0_ref, mine_ref, sem)
+    load.start()
     odd = lax.axis_index("gy") % 2 == 1
     ext[0:4, 4:12, :] = choose(odd, innery_ref[...], outery_ref[...])
     ext[4:8, 4:12, :] = own_ref[...]
@@ -103,6 +105,7 @@
         for x in range(TX):
             slot = assign_ref[y, x]
             rows_ref[slot // SLOTS, pl.ds(slot & (SLOTS - 1), 1), :] = forcing[x : x + 1]
+    load.wait()
 
 
 def split(value):
@@ -132,11 +135,8 @@
     held,
     weights,
     staged,
-    mine,
     sems,
 ):
-    load = pltpu.make_async_copy(r0_ref, mine, sems.at[PAIRS])
-    load.start()
     me = lax.axis_index("ha")
     for x in range(TX):
         for y in range(TY):
@@ -152,7 +152,7 @@
     to_left = half | ((lane8 + WIDTH - 1) & (WIDTH - 1))
     slot_row = lax.broadcasted_iota(jnp.int32, (SLOTS, LANES), 0)
     slot_pair = lax.broadcasted_iota(jnp.int32, (SLOTS, LANES), 1) // WIDTH
-    arrived = (mine, r1_ref, r2_ref, r3_ref)
+    arrived = (r0_ref, r1_ref, r2_ref, r3_ref)
 
     def ends(ref):
         for f in range(FIELDS):
@@ -245,7 +245,6 @@
         one_pair(pair, pair)
         return 0
 
-    load.wait()
     lax.fori_loop(0, PAIRS, each, 0)
     for pair in range(PAIRS):
         send(pair, pair).wait()
@@ -293,8 +292,8 @@
         ],
         compiler_params=pltpu.CompilerParams(vmem_limit_bytes=60 * 1024 * 1024),
     )(assignment, crm_state.reshape(ROWS * TX, TY * WIDTH))
-    *slotted, outer = lax.optimization_barrier((*slotted, outer))
-    arrived = [slotted[0]] + [lax.ppermute(slotted[k], "ha", partners(ORDER[k])) for k in range(1, HELP)]
+    *slotted, outer, inner = lax.optimization_barrier((*slotted, outer, inner))
+    arrived = [lax.ppermute(slotted[k], "ha", partners(ORDER[k])) for k in range(1, HELP)]
 
     edge = jax.ShapeDtypeStruct((3 * TY, 4, LANES), f32)
     to_outer, to_inner = pl.pallas_call(
@@ -308,17 +307,18 @@
     )(own, outer, inner)
     outerx = lax.ppermute(to_outer, "gx", swaps(nx, 1))
     innerx = lax.ppermute(to_inner, "gx", swaps(nx, 0))
-    g4, pushes = pl.pallas_call(
+    g4, pushes, mine = pl.pallas_call(
         forcing_kernel,
         out_shape=[
             jax.ShapeDtypeStruct((TY, TX, LANES), f32),
             jax.ShapeDtypeStruct((HELP, SLOTS, LANES), f32),
+            jax.ShapeDtypeStruct((PAIRS * ROWS, LANES), f32),
         ],
-        in_specs=[smem()] + [vmem()] * 5,
-        out_specs=[vmem()] * 2,
-        scratch_shapes=[pltpu.VMEM((12, 16, LANES), f32)],
+        in_specs=[smem()] + [vmem()] * 5 + [pl.BlockSpec(memory_space=pltpu.HBM)],
+        out_specs=[vmem()] * 3,
+        scratch_shapes=[pltpu.VMEM((12, 16, LANES), f32), pltpu.SemaphoreType.DMA],
         compiler_params=VM,
-    )(assignment, own, outer, inner, outerx, innerx)
+    )(assignment, own, outer, inner, outerx, innerx, slotted[0])
     pushes = lax.all_to_all(pushes, "ha", split_axis=0, concat_axis=0, tiled=True)
 
     final, tendency = pl.pallas_call(
@@ -327,7 +327,7 @@
             jax.ShapeDtypeStruct((LEVELS * FIELDS, SLOTS * WIDTH), f32),
             jax.ShapeDtypeStruct((HELP, SLOTS, LANES), f32),
         ],
-        in_specs=[smem(), smem(), smem()] + [pl.BlockSpec(memory_space=pltpu.HBM)] + [vmem()] * HELP,
+        in_specs=[smem(), smem(), smem()] + [vmem()] * (HELP + 1),
         out_specs=[pl.BlockSpec(memory_space=pltpu.HBM), vmem()],
         scratch_shapes=[
             pltpu.SMEM((COLS,), jnp.int32),
@@ -338,11 +338,10 @@
             pltpu.VMEM((HELP, FIELDS * PITCH, LANES), f32),
             pltpu.VMEM((FIELDS, FIELDS, 8, LANES), f32),
             pltpu.VMEM((PAIRS, LEVELS * FIELDS, LANES), f32),
-            pltpu.VMEM((PAIRS * ROWS, LANES), f32),
-            pltpu.SemaphoreType.DMA((PAIRS + 1,)),
+            pltpu.SemaphoreType.DMA((PAIRS,)),
         ],
         compiler_params=VM,
-    )(assignment, substeps, mixing, *arrived, pushes)
+    )(assignment, substeps, mixing, mine, *arrived, pushes)
     returned = lax.all_to_all(tendency, "ha", split_axis=0, concat_axis=0, tiled=True)
     placed = pl.pallas_call(
         placing_kernel,

time: 112 us -> 113 us (level)
  the two profiles are of different devices: /device:TPU:6 before, /device:TPU:2 now
where the time goes in v5:
time: 113 us; the launch traced here: 112 us
  blocking collectives  46.8 us (41%)
  starting transfers between devices  44.2 us (39%)
  Pallas kernels  16.7 us (15%)
  local copies, waits for them, and re-layouts  2.72 us (2%)
    all_to_all x1, blocking collectives, on_device(): lax.all_to_all(pushes, 'ha', split_axis=0, concat_axis=0, tiled=True)  31.9 us
    ppermute x3, starting transfers between devices, on_device(): lax.ppermute(slotted[k], 'ha', partners(ORDER[k]))  24.7 us
    all_to_all x1, blocking collectives, on_device(): lax.all_to_all(tendency, 'ha', split_axis=0, concat_axis=0, tiled=True)  14.9 us
    pallas_call x1, Pallas kernels, on_device(): pl.pallas_call(advance_kernel, out_shape=[jax.ShapeDtypeStruct((LEVELS *...  10.7 us
    ppermute x1, starting transfers between devices, on_device(): outer = lax.ppermute(own, 'gy', swaps(ny, 1))  10.6 us
    ppermute x1, starting transfers between devices, on_device(): innerx = lax.ppermute(to_inner, 'gx', swaps(nx, 0))  3.5 us
    ppermute x1, starting transfers between devices, on_device(): inner = lax.ppermute(own, 'gy', swaps(ny, 0))  3.48 us
    pallas_call x1, Pallas kernels, on_device(): pl.pallas_call(slotting_kernel, out_shape=[jax.ShapeDtypeStruct((PAIRS *...  3.44 us
  transfers between devices with their start and end apart: 7, of which 1 were waited for; matrix products, arithmetic and copies ran while one was open for 0% of the time, Pallas kernels for 4%

profile of v5, /device:TPU:2, one launch (start us, length us, event | category | flops | bytes accessed | tf_op | source)
XLA Modules:
  0.0 112.1 jit_solution(16013438897261448582)
XLA Ops:
  0.6 0.9 pad_bitcast_fusion
  1.6 0.1 copy.7
  1.7 0.1 reshape.16.own_ref
  1.8 3.5 %collective-permute-start.1 = (f32[4,8,128]{2,1,0:T(8,128)S(1)}, f32[4,8,128]{2,1,0:T(8,128)S(1)}, u32[]{:S(2)}, u32[]{:S(2)}) collective-permute-start(f32[4,8,128]{2,1,0:T(8,128)S(1)} %reshape.16.own_ref), channel_id=1, source_target_pairs={{0,4},{8,12},{16,20},{24,28},{32,36},{40,44},{48,52},{56,60},{64,6... | collective-permute-start | bytes 49160 | tf_op jit(solution)/shard_map/ppermute | solution.py:281
  5.3 10.6 %collective-permute-start = (f32[4,8,128]{2,1,0:T(8,128)S(1)}, f32[4,8,128]{2,1,0:T(8,128)S(1)}, u32[]{:S(2)}, u32[]{:S(2)}) collective-permute-start(f32[4,8,128]{2,1,0:T(8,128)S(1)} %reshape.16.own_ref), channel_id=1, source_target_pairs={{4,8},{12,16},{20,24},{28,32},{36,40},{44,48},{52,56},{60,64},{68,... | collective-permute-start | bytes 49160 | tf_op jit(solution)/shard_map/ppermute | solution.py:280
  15.8 3.4 %shard_map.68 = (f32[480,128]{1,0:T(8,128)}, f32[480,128]{1,0:T(8,128)}, f32[480,128]{1,0:T(8,128)}, f32[480,128]{1,0:T(8,128)}) custom-call(s32[4,8]{1,0:T(4,128)} %bitcast.13, f32[960,256]{1,0:T(8,128)} %bitcast.18), custom_call_target="tpu_custom_call" | custom-call | tf_op jit(solution)/shard_map/pallas_call | solution.py:283
  19.3 0.0 collective-permute-done.1.inner_ref.innery_ref
  19.3 0.0 collective-permute-done.outer_ref.outery_ref
  19.3 16.7 %collective-permute-start.4 = (f32[480,128]{1,0:T(8,128)}, f32[480,128]{1,0:T(8,128)S(1)}, u32[]{:S(2)}, u32[]{:S(2)}) collective-permute-start(f32[480,128]{1,0:T(8,128)} %get-tuple-element.30), channel_id=1, source_target_pairs={{0,2},{1,3},{2,0},{3,1},{4,6},{5,7},{6,4},{7,5},{8,10},{9,11},{10,... | collective-permute-start | bytes 737288 | tf_op jit(solution)/shard_map/ppermute | solution.py:296
  36.0 6.1 %collective-permute-start.5 = (f32[480,128]{1,0:T(8,128)}, f32[480,128]{1,0:T(8,128)S(1)}, u32[]{:S(2)}, u32[]{:S(2)}) collective-permute-start(f32[480,128]{1,0:T(8,128)} %get-tuple-element.31), channel_id=1, source_target_pairs={{0,1},{1,0},{2,3},{3,2},{4,5},{5,4},{6,7},{7,6},{8,9},{9,8},{10,11... | collective-permute-start | bytes 737288 | tf_op jit(solution)/shard_map/ppermute | solution.py:296
  42.1 1.9 %collective-permute-start.6 = (f32[480,128]{1,0:T(8,128)}, f32[480,128]{1,0:T(8,128)S(1)}, u32[]{:S(2)}, u32[]{:S(2)}) collective-permute-start(f32[480,128]{1,0:T(8,128)} %get-tuple-element.32), channel_id=1, source_target_pairs={{0,3},{1,2},{2,1},{3,0},{4,7},{5,6},{6,5},{7,4},{8,11},{9,10},{10,... | collective-permute-start | bytes 737288 | tf_op jit(solution)/shard_map/ppermute | solution.py:296
  44.1 0.0 copy-start.1
  44.1 1.9 %collective-permute-start.2 = (f32[12,4,128]{2,1,0:T(4,128)S(1)}, f32[12,4,128]{2,1,0:T(4,128)S(1)}, u32[]{:S(2)}, u32[]{:S(2)}) collective-permute-start(f32[12,4,128]{2,1,0:T(4,128)S(1)} %get-tuple-element.25), channel_id=1, source_target_pairs={{128,256},{384,512},{640,768},{896,0},{256,128},{512,384},{768,640... | collective-permute-start | bytes 73736 | tf_op jit(solution)/shard_map/ppermute | solution.py:308
  46.0 3.5 %collective-permute-start.3 = (f32[12,4,128]{2,1,0:T(4,128)S(1)}, f32[12,4,128]{2,1,0:T(4,128)S(1)}, u32[]{:S(2)}, u32[]{:S(2)}) collective-permute-start(f32[12,4,128]{2,1,0:T(4,128)S(1)} %get-tuple-element.26), channel_id=1, source_target_pairs={{0,128},{256,384},{512,640},{768,896},{128,0},{384,256},{640,512},... | collective-permute-start | bytes 73736 | tf_op jit(solution)/shard_map/ppermute | solution.py:309
  49.5 0.0 collective-permute-done.2.outerx_ref
  49.5 0.8 collective-permute-done.3.innerx_ref
  50.3 0.0 copy-done.1
  50.3 0.0 copy-start
  50.3 0.9 copy-done
  51.3 1.2 %shard_map.70 = (f32[4,8,128]{2,1,0:T(8,128)S(1)}, f32[4,8,128]{2,1,0:T(8,128)S(1)}, f32[480,128]{1,0:T(8,128)S(1)}) custom-call(s32[4,8]{1,0:T(4,128)S(1)} %bitcast.14, f32[4,8,128]{2,1,0:T(8,128)S(1)} %reshape.16.own_ref, f32[4,8,128]{2,1,0:T(8,128)S(1)} %collective-permute-done.outer_ref.outery_ref, ...), custom_call_target="tpu_custom_call" | custom-call | tf_op jit(solution)/shard_map/pallas_call | solution.py:310
  52.5 0.0 copy-start.2
  52.5 31.9 %all_to_all.10.push_ref = f32[4,8,128]{2,1,0:T(8,128)S(1)} all-to-all(f32[4,8,128]{2,1,0:T(8,128)S(1)} %get-tuple-element.33), channel_id=1, replica_groups=mesh['gx'=8,'gy'=32,'ha'=4] {'ha'}, dimensions={0} | all-to-all | bytes 32768 | tf_op jit(solution)/shard_map/all_to_all | solution.py:322
  84.4 0.0 copy-start.3
  84.4 0.0 collective-permute-done.4.r1_ref
  84.4 0.0 collective-permute-done.5.r2_ref
  84.4 0.0 collective-permute-done.6.r3_ref
  84.4 0.0 copy-done.2
  84.4 0.7 copy-done.3
  85.1 10.7 %shard_map.71 = (f32[480,512]{1,0:T(8,128)}, f32[4,8,128]{2,1,0:T(8,128)S(1)}) custom-call(s32[4,8]{1,0:T(4,128)S(1)} %bitcast.15, s32[4,8]{1,0:T(4,128)S(1)} %bitcast.17, f32[8,8]{1,0:T(8,128)S(1)} %copy-done.2, f32[480,128]{1,0:T(8,128)S(1)} %get-tuple-element.29.r0_ref, f32[480,128]{1,0:T(8,128)S(1)} %collective-permute-done.4.r1_ref, ...), custom_call_target="tpu_custom_call" | custom-call | tf_op jit(solution)/shard_map/pallas_call | solution.py:324
  95.8 14.9 %all_to_all.11 = f32[4,8,128]{2,1,0:T(8,128)S(1)} all-to-all(f32[4,8,128]{2,1,0:T(8,128)S(1)} %get-tuple-element.34), channel_id=1, replica_groups=mesh['gx'=8,'gy'=32,'ha'=4] {'ha'}, dimensions={0} | all-to-all | bytes 32768 | tf_op jit(solution)/shard_map/all_to_all | solution.py:345
  110.7 1.4 %shard_map.72 = f32[8,8,4,15]{3,2,1,0:T(4,128)} custom-call(s32[4,8]{1,0:T(4,128)S(1)} %bitcast.16, f32[4,8,128]{2,1,0:T(8,128)S(1)} %get-tuple-element.28.g4_ref, f32[32,128]{1,0:T(8,128)S(1)} %bitcast.12), custom_call_target="tpu_custom_call" | custom-call | tf_op jit(solution)/shard_map/pallas_call | solution.py:346
  (1 shorter events, 0.0 us)
Async XLA Ops:
  1.8 17.5 %collective-permute-start.1 = (f32[4,8,128]{2,1,0:T(8,128)S(1)}, f32[4,8,128]{2,1,0:T(8,128)S(1)}, u32[]{:S(2)}, u32[]{:S(2)}) collective-permute-start(f32[4,8,128]{2,1,0:T(8,128)S(1)} %reshape.16.own_ref), channel_id=1, source_target_pairs={{0,4},{8,12},{16,20},{24,28},{32,36},{40,44},{48,52},{56,60},{64,6... | collective-permute-start | bytes 49160 | tf_op jit(solution)/shard_map/ppermute | solution.py:281
  5.3 14.0 %collective-permute-start = (f32[4,8,128]{2,1,0:T(8,128)S(1)}, f32[4,8,128]{2,1,0:T(8,128)S(1)}, u32[]{:S(2)}, u32[]{:S(2)}) collective-permute-start(f32[4,8,128]{2,1,0:T(8,128)S(1)} %reshape.16.own_ref), channel_id=1, source_target_pairs={{4,8},{12,16},{20,24},{28,32},{36,40},{44,48},{52,56},{60,64},{68,... | collective-permute-start | bytes 49160 | tf_op jit(solution)/shard_map/ppermute | solution.py:280
  19.3 65.1 %collective-permute-start.4 = (f32[480,128]{1,0:T(8,128)}, f32[480,128]{1,0:T(8,128)S(1)}, u32[]{:S(2)}, u32[]{:S(2)}) collective-permute-start(f32[480,128]{1,0:T(8,128)} %get-tuple-element.30), channel_id=1, source_target_pairs={{0,2},{1,3},{2,0},{3,1},{4,6},{5,7},{6,4},{7,5},{8,10},{9,11},{10,... | collective-permute-start | bytes 737288 | tf_op jit(solution)/shard_map/ppermute | solution.py:296
  36.0 48.4 %collective-permute-start.5 = (f32[480,128]{1,0:T(8,128)}, f32[480,128]{1,0:T(8,128)S(1)}, u32[]{:S(2)}, u32[]{:S(2)}) collective-permute-start(f32[480,128]{1,0:T(8,128)} %get-tuple-element.31), channel_id=1, source_target_pairs={{0,1},{1,0},{2,3},{3,2},{4,5},{5,4},{6,7},{7,6},{8,9},{9,8},{10,11... | collective-permute-start | bytes 737288 | tf_op jit(solution)/shard_map/ppermute | solution.py:296
  42.1 42.3 %collective-permute-start.6 = (f32[480,128]{1,0:T(8,128)}, f32[480,128]{1,0:T(8,128)S(1)}, u32[]{:S(2)}, u32[]{:S(2)}) collective-permute-start(f32[480,128]{1,0:T(8,128)} %get-tuple-element.32), channel_id=1, source_target_pairs={{0,3},{1,2},{2,1},{3,0},{4,7},{5,6},{6,5},{7,4},{8,11},{9,10},{10,... | collective-permute-start | bytes 737288 | tf_op jit(solution)/shard_map/ppermute | solution.py:296
  44.1 6.3 %copy-start.1 = (s32[8,4]{0,1:T(4,128)S(1)}, s32[8,4]{0,1:T(4,128)}, u32[]{:S(2)}) copy-start(s32[8,4]{0,1:T(4,128)} %param.9) | copy-start | bytes 388
  44.1 5.4 %collective-permute-start.2 = (f32[12,4,128]{2,1,0:T(4,128)S(1)}, f32[12,4,128]{2,1,0:T(4,128)S(1)}, u32[]{:S(2)}, u32[]{:S(2)}) collective-permute-start(f32[12,4,128]{2,1,0:T(4,128)S(1)} %get-tuple-element.25), channel_id=1, source_target_pairs={{128,256},{384,512},{640,768},{896,0},{256,128},{512,384},{768,640... | collective-permute-start | bytes 73736 | tf_op jit(solution)/shard_map/ppermute | solution.py:308
  46.0 4.3 %collective-permute-start.3 = (f32[12,4,128]{2,1,0:T(4,128)S(1)}, f32[12,4,128]{2,1,0:T(4,128)S(1)}, u32[]{:S(2)}, u32[]{:S(2)}) collective-permute-start(f32[12,4,128]{2,1,0:T(4,128)S(1)} %get-tuple-element.26), channel_id=1, source_target_pairs={{0,128},{256,384},{512,640},{768,896},{128,0},{384,256},{640,512},... | collective-permute-start | bytes 73736 | tf_op jit(solution)/shard_map/ppermute | solution.py:309
  50.3 0.9 copy-start
  52.5 31.9 %copy-start.2 = (f32[8,8]{1,0:T(8,128)S(1)}, f32[8,8]{1,0:T(8,128)}, u32[]{:S(2)}) copy-start(f32[8,8]{1,0:T(8,128)} %mix_ref.1) | copy-start | bytes 772
  84.4 0.7 copy-start.3

commit v6 on v5

--- a/solution.py
+++ b/solution.py
@@ -79,7 +79,7 @@
     to_inner_ref[...] = choose(odd, low, high)
 
 
-def forcing_kernel(assign_ref, own_ref, outery_ref, innery_ref, outerx_ref, innerx_ref, s0_ref, g4_ref, rows_ref, mine_ref, ext, sem):
+def forcing_kernel(assign_ref, sub_ref, own_ref, outery_ref, innery_ref, outerx_ref, innerx_ref, s0_ref, g4_ref, rows_ref, mine_ref, counts_ref, ext, sem):
     load = pltpu.make_async_copy(s0_ref, mine_ref, sem)
     load.start()
     odd = lax.axis_index("gy") % 2 == 1
@@ -105,6 +105,7 @@
         for x in range(TX):
             slot = assign_ref[y, x]
             rows_ref[slot // SLOTS, pl.ds(slot & (SLOTS - 1), 1), :] = forcing[x : x + 1]
+            counts_ref[slot] = sub_ref[y, x]
     load.wait()
 
 
@@ -117,8 +118,7 @@
 
 
 def advance_kernel(
-    assign_ref,
-    sub_ref,
+    counts,
     mix_ref,
     r0_ref,
     r1_ref,
@@ -127,7 +127,6 @@
     push_ref,
     out_ref,
     tend_ref,
-    counts,
     one,
     two,
     push,
@@ -138,9 +137,6 @@
     sems,
 ):
     me = lax.axis_index("ha")
-    for x in range(TX):
-        for y in range(TY):
-            counts[assign_ref[y, x]] = sub_ref[y, x]
     tend_ref[...] = jnp.zeros_like(tend_ref)
     gather[...] = jnp.zeros_like(gather)
     for h in range(FIELDS):
@@ -292,7 +288,7 @@
         ],
         compiler_params=pltpu.CompilerParams(vmem_limit_bytes=60 * 1024 * 1024),
     )(assignment, crm_state.reshape(ROWS * TX, TY * WIDTH))
-    *slotted, outer, inner = lax.optimization_barrier((*slotted, outer, inner))
+    *slotted, inner, outer = lax.optimization_barrier((*slotted, inner, outer))
     arrived = [lax.ppermute(slotted[k], "ha", partners(ORDER[k])) for k in range(1, HELP)]
 
     edge = jax.ShapeDtypeStruct((3 * TY, 4, LANES), f32)
@@ -307,18 +303,19 @@
     )(own, outer, inner)
     outerx = lax.ppermute(to_outer, "gx", swaps(nx, 1))
     innerx = lax.ppermute(to_inner, "gx", swaps(nx, 0))
-    g4, pushes, mine = pl.pallas_call(
+    g4, pushes, mine, counts = pl.pallas_call(
         forcing_kernel,
         out_shape=[
             jax.ShapeDtypeStruct((TY, TX, LANES), f32),
             jax.ShapeDtypeStruct((HELP, SLOTS, LANES), f32),
             jax.ShapeDtypeStruct((PAIRS * ROWS, LANES), f32),
+            jax.ShapeDtypeStruct((COLS,), jnp.int32),
         ],
-        in_specs=[smem()] + [vmem()] * 5 + [pl.BlockSpec(memory_space=pltpu.HBM)],
-        out_specs=[vmem()] * 3,
+        in_specs=[smem(), smem()] + [vmem()] * 5 + [pl.BlockSpec(memory_space=pltpu.HBM)],
+        out_specs=[vmem()] * 3 + [smem()],
         scratch_shapes=[pltpu.VMEM((12, 16, LANES), f32), pltpu.SemaphoreType.DMA],
         compiler_params=VM,
-    )(assignment, own, outer, inner, outerx, innerx, slotted[0])
+    )(assignment, substeps, own, outer, inner, outerx, innerx, slotted[0])
     pushes = lax.all_to_all(pushes, "ha", split_axis=0, concat_axis=0, tiled=True)
 
     final, tendency = pl.pallas_call(
@@ -327,10 +324,9 @@
             jax.ShapeDtypeStruct((LEVELS * FIELDS, SLOTS * WIDTH), f32),
             jax.ShapeDtypeStruct((HELP, SLOTS, LANES), f32),
         ],
-        in_specs=[smem(), smem(), smem()] + [vmem()] * (HELP + 1),
+        in_specs=[smem(), smem()] + [vmem()] * (HELP + 1),
         out_specs=[pl.BlockSpec(memory_space=pltpu.HBM), vmem()],
         scratch_shapes=[
-            pltpu.SMEM((COLS,), jnp.int32),
             pltpu.VMEM((FIELDS, SROWS, LANES), f32),
             pltpu.VMEM((FIELDS, SROWS, LANES), f32),
             pltpu.VMEM((FIELDS, 64, LANES), f32),
@@ -341,7 +337,7 @@
             pltpu.SemaphoreType.DMA((PAIRS,)),
         ],
         compiler_params=VM,
-    )(assignment, substeps, mixing, mine, *arrived, pushes)
+    )(counts, mixing, mine, *arrived, pushes)
     returned = lax.all_to_all(tendency, "ha", split_axis=0, concat_axis=0, tiled=True)
     placed = pl.pallas_call(
         placing_kernel,

time: 113 us -> 111 us (0.982)
  the two profiles are of different devices: /device:TPU:2 before, /device:TPU:6 now
where the time goes in v6:
time: 111 us; the launch traced here: 109 us
  blocking collectives  47.3 us (43%)
  starting transfers between devices  41.8 us (38%)
  Pallas kernels  15.7 us (14%)
  local copies, waits for them, and re-layouts  2.08 us (2%)
    all_to_all x1, blocking collectives, on_device(): lax.all_to_all(pushes, 'ha', split_axis=0, concat_axis=0, tiled=True)  32.3 us
    ppermute x3, starting transfers between devices, on_device(): lax.ppermute(slotted[k], 'ha', partners(ORDER[k]))  24.7 us
    all_to_all x1, blocking collectives, on_device(): lax.all_to_all(tendency, 'ha', split_axis=0, concat_axis=0, tiled=True)  15 us
    ppermute x1, starting transfers between devices, on_device(): outer = lax.ppermute(own, 'gy', swaps(ny, 1))  10.8 us
    pallas_call x1, Pallas kernels, on_device(): pl.pallas_call(advance_kernel, out_shape=[jax.ShapeDtypeStruct((LEVELS *...  9.06 us
    pallas_call x1, Pallas kernels, on_device(): pl.pallas_call(slotting_kernel, out_shape=[jax.ShapeDtypeStruct((PAIRS *...  3.44 us
    ppermute x1, starting transfers between devices, on_device(): innerx = lax.ppermute(to_inner, 'gx', swaps(nx, 0))  2.49 us
  transfers between devices with their start and end apart: 7, of which 3 were waited for; matrix products, arithmetic and copies ran while one was open for 0% of the time, Pallas kernels for 5%

profile of v6, /device:TPU:6, one launch (start us, length us, event | category | flops | bytes accessed | tf_op | source)
XLA Modules:
  0.0 108.7 jit_solution(1154361415166802411)
XLA Ops:
  0.6 0.9 pad_bitcast_fusion
  1.6 0.1 copy.7
  1.7 0.1 reshape.16.own_ref
  1.8 10.8 %collective-permute-start.1 = (f32[4,8,128]{2,1,0:T(8,128)S(1)}, f32[4,8,128]{2,1,0:T(8,128)S(1)}, u32[]{:S(2)}, u32[]{:S(2)}) collective-permute-start(f32[4,8,128]{2,1,0:T(8,128)S(1)} %reshape.16.own_ref), channel_id=1, source_target_pairs={{4,8},{12,16},{20,24},{28,32},{36,40},{44,48},{52,56},{60,64},{68,... | collective-permute-start | bytes 49160 | tf_op jit(solution)/shard_map/ppermute | solution.py:276
  12.6 1.9 %collective-permute-start = (f32[4,8,128]{2,1,0:T(8,128)S(1)}, f32[4,8,128]{2,1,0:T(8,128)S(1)}, u32[]{:S(2)}, u32[]{:S(2)}) collective-permute-start(f32[4,8,128]{2,1,0:T(8,128)S(1)} %reshape.16.own_ref), channel_id=1, source_target_pairs={{0,4},{8,12},{16,20},{24,28},{32,36},{40,44},{48,52},{56,60},{64,6... | collective-permute-start | bytes 49160 | tf_op jit(solution)/shard_map/ppermute | solution.py:277
  14.5 3.4 %shard_map.68 = (f32[480,128]{1,0:T(8,128)}, f32[480,128]{1,0:T(8,128)}, f32[480,128]{1,0:T(8,128)}, f32[480,128]{1,0:T(8,128)}) custom-call(s32[4,8]{1,0:T(4,128)} %bitcast.13, f32[960,256]{1,0:T(8,128)} %bitcast.17), custom_call_target="tpu_custom_call" | custom-call | tf_op jit(solution)/shard_map/pallas_call | solution.py:279
  17.9 0.0 collective-permute-done.1.outer_ref.outery_ref
  18.0 0.2 collective-permute-done.inner_ref.innery_ref
  18.2 16.7 %collective-permute-start.4 = (f32[480,128]{1,0:T(8,128)}, f32[480,128]{1,0:T(8,128)S(1)}, u32[]{:S(2)}, u32[]{:S(2)}) collective-permute-start(f32[480,128]{1,0:T(8,128)} %get-tuple-element.32), channel_id=1, source_target_pairs={{0,2},{1,3},{2,0},{3,1},{4,6},{5,7},{6,4},{7,5},{8,10},{9,11},{10,... | collective-permute-start | bytes 737288 | tf_op jit(solution)/shard_map/ppermute | solution.py:292
  34.9 6.1 %collective-permute-start.5 = (f32[480,128]{1,0:T(8,128)}, f32[480,128]{1,0:T(8,128)S(1)}, u32[]{:S(2)}, u32[]{:S(2)}) collective-permute-start(f32[480,128]{1,0:T(8,128)} %get-tuple-element.33), channel_id=1, source_target_pairs={{0,1},{1,0},{2,3},{3,2},{4,5},{5,4},{6,7},{7,6},{8,9},{9,8},{10,11... | collective-permute-start | bytes 737288 | tf_op jit(solution)/shard_map/ppermute | solution.py:292
  41.0 1.9 %collective-permute-start.6 = (f32[480,128]{1,0:T(8,128)}, f32[480,128]{1,0:T(8,128)S(1)}, u32[]{:S(2)}, u32[]{:S(2)}) collective-permute-start(f32[480,128]{1,0:T(8,128)} %get-tuple-element.34), channel_id=1, source_target_pairs={{0,3},{1,2},{2,1},{3,0},{4,7},{5,6},{6,5},{7,4},{8,11},{9,10},{10,... | collective-permute-start | bytes 737288 | tf_op jit(solution)/shard_map/ppermute | solution.py:292
  42.9 0.0 copy-start.3
  43.0 0.0 copy-start.1
  43.0 1.9 %collective-permute-start.2 = (f32[12,4,128]{2,1,0:T(4,128)S(1)}, f32[12,4,128]{2,1,0:T(4,128)S(1)}, u32[]{:S(2)}, u32[]{:S(2)}) collective-permute-start(f32[12,4,128]{2,1,0:T(4,128)S(1)} %get-tuple-element.26), channel_id=1, source_target_pairs={{128,256},{384,512},{640,768},{896,0},{256,128},{512,384},{768,640... | collective-permute-start | bytes 73736 | tf_op jit(solution)/shard_map/ppermute | solution.py:304
  44.9 2.5 %collective-permute-start.3 = (f32[12,4,128]{2,1,0:T(4,128)S(1)}, f32[12,4,128]{2,1,0:T(4,128)S(1)}, u32[]{:S(2)}, u32[]{:S(2)}) collective-permute-start(f32[12,4,128]{2,1,0:T(4,128)S(1)} %get-tuple-element.27), channel_id=1, source_target_pairs={{0,128},{256,384},{512,640},{768,896},{128,0},{384,256},{640,512},... | collective-permute-start | bytes 73736 | tf_op jit(solution)/shard_map/ppermute | solution.py:305
  47.4 0.7 collective-permute-done.2.outerx_ref
  48.1 0.1 collective-permute-done.3.innerx_ref
  48.2 0.0 copy-done.3
  48.2 0.0 copy-done.1
  48.2 0.0 copy-start
  48.2 0.9 copy-done
  49.2 1.8 %shard_map.70 = (f32[4,8,128]{2,1,0:T(8,128)S(1)}, f32[4,8,128]{2,1,0:T(8,128)S(1)}, f32[480,128]{1,0:T(8,128)S(1)}, s32[32]{0:T(128)S(1)}) custom-call(s32[4,8]{1,0:T(4,128)S(1)} %bitcast.14, s32[4,8]{1,0:T(4,128)S(1)} %bitcast.16, f32[4,8,128]{2,1,0:T(8,128)S(1)} %reshape.16.own_ref, f32[4,8,128]{2,1,0:T(8,128)S(1)} %collective-permute-done.1.outer_ref.outery_ref, ...), custom_call_target="tpu_custom_call" | custom-call | tf_op jit(solution)/shard_map/pallas_call | solution.py:306
  51.0 0.0 copy-start.2
  51.0 32.3 %all_to_all.10.push_ref = f32[4,8,128]{2,1,0:T(8,128)S(1)} all-to-all(f32[4,8,128]{2,1,0:T(8,128)S(1)} %get-tuple-element.35), channel_id=1, replica_groups=mesh['gx'=8,'gy'=32,'ha'=4] {'ha'}, dimensions={0} | all-to-all | bytes 32768 | tf_op jit(solution)/shard_map/all_to_all | solution.py:319
  83.3 0.0 collective-permute-done.4.r1_ref
  83.3 0.0 collective-permute-done.5.r2_ref
  83.3 0.0 collective-permute-done.6.r3_ref
  83.3 0.0 copy-done.2
  83.3 9.1 %shard_map.71 = (f32[480,512]{1,0:T(8,128)}, f32[4,8,128]{2,1,0:T(8,128)S(1)}) custom-call(s32[32]{0:T(128)S(1)} %get-tuple-element.30.counts, f32[8,8]{1,0:T(8,128)S(1)} %copy-done.2, f32[480,128]{1,0:T(8,128)S(1)} %get-tuple-element.31.r0_ref, f32[480,128]{1,0:T(8,128)S(1)} %collective-permute-done.4.r1_ref, f32[480,128]{1,0:T(8,128)S(1)} %collective-permute-done.5.r2_ref, ...), custom_call_target="tpu_custom_call" | custom-call | tf_op jit(solution)/shard_map/pallas_call | solution.py:321
  92.4 15.0 %all_to_all.11 = f32[4,8,128]{2,1,0:T(8,128)S(1)} all-to-all(f32[4,8,128]{2,1,0:T(8,128)S(1)} %get-tuple-element.36), channel_id=1, replica_groups=mesh['gx'=8,'gy'=32,'ha'=4] {'ha'}, dimensions={0} | all-to-all | bytes 32768 | tf_op jit(solution)/shard_map/all_to_all | solution.py:341
  107.4 1.4 %shard_map.72 = f32[8,8,4,15]{3,2,1,0:T(4,128)} custom-call(s32[4,8]{1,0:T(4,128)S(1)} %bitcast.15, f32[4,8,128]{2,1,0:T(8,128)S(1)} %get-tuple-element.29.g4_ref, f32[32,128]{1,0:T(8,128)S(1)} %bitcast.12), custom_call_target="tpu_custom_call" | custom-call | tf_op jit(solution)/shard_map/pallas_call | solution.py:342
  (1 shorter events, 0.0 us)
Async XLA Ops:
  1.8 16.2 %collective-permute-start.1 = (f32[4,8,128]{2,1,0:T(8,128)S(1)}, f32[4,8,128]{2,1,0:T(8,128)S(1)}, u32[]{:S(2)}, u32[]{:S(2)}) collective-permute-start(f32[4,8,128]{2,1,0:T(8,128)S(1)} %reshape.16.own_ref), channel_id=1, source_target_pairs={{4,8},{12,16},{20,24},{28,32},{36,40},{44,48},{52,56},{60,64},{68,... | collective-permute-start | bytes 49160 | tf_op jit(solution)/shard_map/ppermute | solution.py:276
  12.6 5.6 %collective-permute-start = (f32[4,8,128]{2,1,0:T(8,128)S(1)}, f32[4,8,128]{2,1,0:T(8,128)S(1)}, u32[]{:S(2)}, u32[]{:S(2)}) collective-permute-start(f32[4,8,128]{2,1,0:T(8,128)S(1)} %reshape.16.own_ref), channel_id=1, source_target_pairs={{0,4},{8,12},{16,20},{24,28},{32,36},{40,44},{48,52},{56,60},{64,6... | collective-permute-start | bytes 49160 | tf_op jit(solution)/shard_map/ppermute | solution.py:277
  18.2 65.1 %collective-permute-start.4 = (f32[480,128]{1,0:T(8,128)}, f32[480,128]{1,0:T(8,128)S(1)}, u32[]{:S(2)}, u32[]{:S(2)}) collective-permute-start(f32[480,128]{1,0:T(8,128)} %get-tuple-element.32), channel_id=1, source_target_pairs={{0,2},{1,3},{2,0},{3,1},{4,6},{5,7},{6,4},{7,5},{8,10},{9,11},{10,... | collective-permute-start | bytes 737288 | tf_op jit(solution)/shard_map/ppermute | solution.py:292
  34.9 48.4 %collective-permute-start.5 = (f32[480,128]{1,0:T(8,128)}, f32[480,128]{1,0:T(8,128)S(1)}, u32[]{:S(2)}, u32[]{:S(2)}) collective-permute-start(f32[480,128]{1,0:T(8,128)} %get-tuple-element.33), channel_id=1, source_target_pairs={{0,1},{1,0},{2,3},{3,2},{4,5},{5,4},{6,7},{7,6},{8,9},{9,8},{10,11... | collective-permute-start | bytes 737288 | tf_op jit(solution)/shard_map/ppermute | solution.py:292
  41.0 42.3 %collective-permute-start.6 = (f32[480,128]{1,0:T(8,128)}, f32[480,128]{1,0:T(8,128)S(1)}, u32[]{:S(2)}, u32[]{:S(2)}) collective-permute-start(f32[480,128]{1,0:T(8,128)} %get-tuple-element.34), channel_id=1, source_target_pairs={{0,3},{1,2},{2,1},{3,0},{4,7},{5,6},{6,5},{7,4},{8,11},{9,10},{10,... | collective-permute-start | bytes 737288 | tf_op jit(solution)/shard_map/ppermute | solution.py:292
  42.9 5.3 %copy-start.3 = (s32[8,4]{0,1:T(4,128)S(1)}, s32[8,4]{0,1:T(4,128)}, u32[]{:S(2)}) copy-start(s32[8,4]{0,1:T(4,128)} %param.8) | copy-start | bytes 388
  43.0 5.3 %copy-start.1 = (s32[8,4]{0,1:T(4,128)S(1)}, s32[8,4]{0,1:T(4,128)}, u32[]{:S(2)}) copy-start(s32[8,4]{0,1:T(4,128)} %param.9) | copy-start | bytes 388
  43.0 5.1 %collective-permute-start.2 = (f32[12,4,128]{2,1,0:T(4,128)S(1)}, f32[12,4,128]{2,1,0:T(4,128)S(1)}, u32[]{:S(2)}, u32[]{:S(2)}) collective-permute-start(f32[12,4,128]{2,1,0:T(4,128)S(1)} %get-tuple-element.26), channel_id=1, source_target_pairs={{128,256},{384,512},{640,768},{896,0},{256,128},{512,384},{768,640... | collective-permute-start | bytes 73736 | tf_op jit(solution)/shard_map/ppermute | solution.py:304
  44.9 3.3 %collective-permute-start.3 = (f32[12,4,128]{2,1,0:T(4,128)S(1)}, f32[12,4,128]{2,1,0:T(4,128)S(1)}, u32[]{:S(2)}, u32[]{:S(2)}) collective-permute-start(f32[12,4,128]{2,1,0:T(4,128)S(1)} %get-tuple-element.27), channel_id=1, source_target_pairs={{0,128},{256,384},{512,640},{768,896},{128,0},{384,256},{640,512},... | collective-permute-start | bytes 73736 | tf_op jit(solution)/shard_map/ppermute | solution.py:305
  48.2 0.9 copy-start
  51.0 32.3 %copy-start.2 = (f32[8,8]{1,0:T(8,128)S(1)}, f32[8,8]{1,0:T(8,128)}, u32[]{:S(2)}) copy-start(f32[8,8]{1,0:T(8,128)} %mix_ref.1) | copy-start | bytes 772

commit v7 on v6

--- a/solution.py
+++ b/solution.py
@@ -49,19 +49,29 @@
             inverse[assign_ref[y, x]] = x * TY + y
     lane = lax.broadcasted_iota(jnp.int32, (ROWS, LANES), 1)
 
-    def column(slot, half):
+    low = jnp.where(lane < WIDTH, 1, 0)
+
+    def column(slot):
         place = inverse[slot]
-        x = place // TY
         y = place % TY
-        rows = held[y // 2, pl.ds(x, ROWS, stride=TX), :]
-        return pltpu.roll(rows, ((y % 2) ^ half) * WIDTH, 1)
+        return held[y // 2, pl.ds(place // TY, ROWS, stride=TX), :], y % 2
+
+    def both(slot):
+        first, at = column(slot)
+        second, to = column(slot + 1)
+        same = jnp.where(at == to, 1, 0)
+        other = low ^ at
+        turned = jnp.where(same == 1, at, other) == 1
+        kept = other + same == 2
+        moved = pltpu.roll(jnp.where(turned, first, second), jnp.where(same == 1, WIDTH, at * WIDTH), 1)
+        return jnp.where(kept, jnp.where(at == 1, second, first), moved)
 
     for load in loads:
         load.wait()
     for k, part in enumerate((s0_ref, s1_ref, s2_ref, s3_ref)):
         for pair in range(PAIRS):
             slot = (me ^ ORDER[k]) * SLOTS + 2 * pair
-            part[pair * ROWS : (pair + 1) * ROWS, :] = jnp.where(lane < WIDTH, column(slot, 0), column(slot + 1, 1))
+            part[pair * ROWS : (pair + 1) * ROWS, :] = both(slot)
 
 
 def choose(odd, first, second):

time: 111 us -> 111 us (level)
  no operation moved by 1% of the time
where the time goes in v7:
time: 111 us; the launch traced here: 109 us
  blocking collectives  47.3 us (43%)
  starting transfers between devices  41.8 us (38%)
  Pallas kernels  16.3 us (15%)
  local copies, waits for them, and re-layouts  2.08 us (2%)
    all_to_all x1, blocking collectives, on_device(): lax.all_to_all(pushes, 'ha', split_axis=0, concat_axis=0, tiled=True)  32.4 us
    ppermute x3, starting transfers between devices, on_device(): lax.ppermute(slotted[k], 'ha', partners(ORDER[k]))  24.7 us
    all_to_all x1, blocking collectives, on_device(): lax.all_to_all(tendency, 'ha', split_axis=0, concat_axis=0, tiled=True)  14.9 us
    ppermute x1, starting transfers between devices, on_device(): outer = lax.ppermute(own, 'gy', swaps(ny, 1))  10.8 us
    pallas_call x1, Pallas kernels, on_device(): pl.pallas_call(advance_kernel, out_shape=[jax.ShapeDtypeStruct((LEVELS *...  9.56 us
    pallas_call x1, Pallas kernels, on_device(): pl.pallas_call(slotting_kernel, out_shape=[jax.ShapeDtypeStruct((PAIRS *...  3.51 us
    ppermute x1, starting transfers between devices, on_device(): innerx = lax.ppermute(to_inner, 'gx', swaps(nx, 0))  2.49 us
  transfers between devices with their start and end apart: 7, of which 3 were waited for; matrix products, arithmetic and copies ran while one was open for 0% of the time, Pallas kernels for 5%

profile of v7, /device:TPU:6, one launch (start us, length us, event | category | flops | bytes accessed | tf_op | source)
XLA Modules:
  0.0 109.3 jit_solution(11584636561394585682)
XLA Ops:
  0.6 0.9 pad_bitcast_fusion
  1.6 0.1 copy.7
  1.7 0.1 reshape.16.own_ref
  1.8 10.8 %collective-permute-start.1 = (f32[4,8,128]{2,1,0:T(8,128)S(1)}, f32[4,8,128]{2,1,0:T(8,128)S(1)}, u32[]{:S(2)}, u32[]{:S(2)}) collective-permute-start(f32[4,8,128]{2,1,0:T(8,128)S(1)} %reshape.16.own_ref), channel_id=1, source_target_pairs={{4,8},{12,16},{20,24},{28,32},{36,40},{44,48},{52,56},{60,64},{68,... | collective-permute-start | bytes 49160 | tf_op jit(solution)/shard_map/ppermute | solution.py:286
  12.6 1.9 %collective-permute-start = (f32[4,8,128]{2,1,0:T(8,128)S(1)}, f32[4,8,128]{2,1,0:T(8,128)S(1)}, u32[]{:S(2)}, u32[]{:S(2)}) collective-permute-start(f32[4,8,128]{2,1,0:T(8,128)S(1)} %reshape.16.own_ref), channel_id=1, source_target_pairs={{0,4},{8,12},{16,20},{24,28},{32,36},{40,44},{48,52},{56,60},{64,6... | collective-permute-start | bytes 49160 | tf_op jit(solution)/shard_map/ppermute | solution.py:287
  14.5 3.5 %shard_map.68 = (f32[480,128]{1,0:T(8,128)}, f32[480,128]{1,0:T(8,128)}, f32[480,128]{1,0:T(8,128)}, f32[480,128]{1,0:T(8,128)}) custom-call(s32[4,8]{1,0:T(4,128)} %bitcast.13, f32[960,256]{1,0:T(8,128)} %bitcast.17), custom_call_target="tpu_custom_call" | custom-call | tf_op jit(solution)/shard_map/pallas_call | solution.py:289
  18.0 0.0 collective-permute-done.1.outer_ref.outery_ref
  18.0 0.2 collective-permute-done.inner_ref.innery_ref
  18.2 16.7 %collective-permute-start.4 = (f32[480,128]{1,0:T(8,128)}, f32[480,128]{1,0:T(8,128)S(1)}, u32[]{:S(2)}, u32[]{:S(2)}) collective-permute-start(f32[480,128]{1,0:T(8,128)} %get-tuple-element.32), channel_id=1, source_target_pairs={{0,2},{1,3},{2,0},{3,1},{4,6},{5,7},{6,4},{7,5},{8,10},{9,11},{10,... | collective-permute-start | bytes 737288 | tf_op jit(solution)/shard_map/ppermute | solution.py:302
  34.9 6.1 %collective-permute-start.5 = (f32[480,128]{1,0:T(8,128)}, f32[480,128]{1,0:T(8,128)S(1)}, u32[]{:S(2)}, u32[]{:S(2)}) collective-permute-start(f32[480,128]{1,0:T(8,128)} %get-tuple-element.33), channel_id=1, source_target_pairs={{0,1},{1,0},{2,3},{3,2},{4,5},{5,4},{6,7},{7,6},{8,9},{9,8},{10,11... | collective-permute-start | bytes 737288 | tf_op jit(solution)/shard_map/ppermute | solution.py:302
  41.0 1.9 %collective-permute-start.6 = (f32[480,128]{1,0:T(8,128)}, f32[480,128]{1,0:T(8,128)S(1)}, u32[]{:S(2)}, u32[]{:S(2)}) collective-permute-start(f32[480,128]{1,0:T(8,128)} %get-tuple-element.34), channel_id=1, source_target_pairs={{0,3},{1,2},{2,1},{3,0},{4,7},{5,6},{6,5},{7,4},{8,11},{9,10},{10,... | collective-permute-start | bytes 737288 | tf_op jit(solution)/shard_map/ppermute | solution.py:302
  42.9 0.0 copy-start.3
  43.0 0.0 copy-start.1
  43.0 1.9 %collective-permute-start.2 = (f32[12,4,128]{2,1,0:T(4,128)S(1)}, f32[12,4,128]{2,1,0:T(4,128)S(1)}, u32[]{:S(2)}, u32[]{:S(2)}) collective-permute-start(f32[12,4,128]{2,1,0:T(4,128)S(1)} %get-tuple-element.26), channel_id=1, source_target_pairs={{128,256},{384,512},{640,768},{896,0},{256,128},{512,384},{768,640... | collective-permute-start | bytes 73736 | tf_op jit(solution)/shard_map/ppermute | solution.py:314
  44.9 2.5 %collective-permute-start.3 = (f32[12,4,128]{2,1,0:T(4,128)S(1)}, f32[12,4,128]{2,1,0:T(4,128)S(1)}, u32[]{:S(2)}, u32[]{:S(2)}) collective-permute-start(f32[12,4,128]{2,1,0:T(4,128)S(1)} %get-tuple-element.27), channel_id=1, source_target_pairs={{0,128},{256,384},{512,640},{768,896},{128,0},{384,256},{640,512},... | collective-permute-start | bytes 73736 | tf_op jit(solution)/shard_map/ppermute | solution.py:315
  47.4 0.7 collective-permute-done.2.outerx_ref
  48.1 0.1 collective-permute-done.3.innerx_ref
  48.2 0.0 copy-done.3
  48.2 0.0 copy-done.1
  48.2 0.0 copy-start
  48.2 0.9 copy-done
  49.2 1.8 %shard_map.70 = (f32[4,8,128]{2,1,0:T(8,128)S(1)}, f32[4,8,128]{2,1,0:T(8,128)S(1)}, f32[480,128]{1,0:T(8,128)S(1)}, s32[32]{0:T(128)S(1)}) custom-call(s32[4,8]{1,0:T(4,128)S(1)} %bitcast.14, s32[4,8]{1,0:T(4,128)S(1)} %bitcast.16, f32[4,8,128]{2,1,0:T(8,128)S(1)} %reshape.16.own_ref, f32[4,8,128]{2,1,0:T(8,128)S(1)} %collective-permute-done.1.outer_ref.outery_ref, ...), custom_call_target="tpu_custom_call" | custom-call | tf_op jit(solution)/shard_map/pallas_call | solution.py:316
  51.0 0.0 copy-start.2
  51.0 32.4 %all_to_all.10.push_ref = f32[4,8,128]{2,1,0:T(8,128)S(1)} all-to-all(f32[4,8,128]{2,1,0:T(8,128)S(1)} %get-tuple-element.35), channel_id=1, replica_groups=mesh['gx'=8,'gy'=32,'ha'=4] {'ha'}, dimensions={0} | all-to-all | bytes 32768 | tf_op jit(solution)/shard_map/all_to_all | solution.py:329
  83.4 0.0 collective-permute-done.4.r1_ref
  83.4 0.0 collective-permute-done.5.r2_ref
  83.4 0.0 collective-permute-done.6.r3_ref
  83.4 0.0 copy-done.2
  83.4 9.6 %shard_map.71 = (f32[480,512]{1,0:T(8,128)}, f32[4,8,128]{2,1,0:T(8,128)S(1)}) custom-call(s32[32]{0:T(128)S(1)} %get-tuple-element.30.counts, f32[8,8]{1,0:T(8,128)S(1)} %copy-done.2, f32[480,128]{1,0:T(8,128)S(1)} %get-tuple-element.31.r0_ref, f32[480,128]{1,0:T(8,128)S(1)} %collective-permute-done.4.r1_ref, f32[480,128]{1,0:T(8,128)S(1)} %collective-permute-done.5.r2_ref, ...), custom_call_target="tpu_custom_call" | custom-call | tf_op jit(solution)/shard_map/pallas_call | solution.py:331
  93.0 14.9 %all_to_all.11 = f32[4,8,128]{2,1,0:T(8,128)S(1)} all-to-all(f32[4,8,128]{2,1,0:T(8,128)S(1)} %get-tuple-element.36), channel_id=1, replica_groups=mesh['gx'=8,'gy'=32,'ha'=4] {'ha'}, dimensions={0} | all-to-all | bytes 32768 | tf_op jit(solution)/shard_map/all_to_all | solution.py:351
  107.9 1.4 %shard_map.72 = f32[8,8,4,15]{3,2,1,0:T(4,128)} custom-call(s32[4,8]{1,0:T(4,128)S(1)} %bitcast.15, f32[4,8,128]{2,1,0:T(8,128)S(1)} %get-tuple-element.29.g4_ref, f32[32,128]{1,0:T(8,128)S(1)} %bitcast.12), custom_call_target="tpu_custom_call" | custom-call | tf_op jit(solution)/shard_map/pallas_call | solution.py:352
  (1 shorter events, 0.0 us)
Async XLA Ops:
  1.8 16.3 %collective-permute-start.1 = (f32[4,8,128]{2,1,0:T(8,128)S(1)}, f32[4,8,128]{2,1,0:T(8,128)S(1)}, u32[]{:S(2)}, u32[]{:S(2)}) collective-permute-start(f32[4,8,128]{2,1,0:T(8,128)S(1)} %reshape.16.own_ref), channel_id=1, source_target_pairs={{4,8},{12,16},{20,24},{28,32},{36,40},{44,48},{52,56},{60,64},{68,... | collective-permute-start | bytes 49160 | tf_op jit(solution)/shard_map/ppermute | solution.py:286
  12.6 5.6 %collective-permute-start = (f32[4,8,128]{2,1,0:T(8,128)S(1)}, f32[4,8,128]{2,1,0:T(8,128)S(1)}, u32[]{:S(2)}, u32[]{:S(2)}) collective-permute-start(f32[4,8,128]{2,1,0:T(8,128)S(1)} %reshape.16.own_ref), channel_id=1, source_target_pairs={{0,4},{8,12},{16,20},{24,28},{32,36},{40,44},{48,52},{56,60},{64,6... | collective-permute-start | bytes 49160 | tf_op jit(solution)/shard_map/ppermute | solution.py:287
  18.2 65.2 %collective-permute-start.4 = (f32[480,128]{1,0:T(8,128)}, f32[480,128]{1,0:T(8,128)S(1)}, u32[]{:S(2)}, u32[]{:S(2)}) collective-permute-start(f32[480,128]{1,0:T(8,128)} %get-tuple-element.32), channel_id=1, source_target_pairs={{0,2},{1,3},{2,0},{3,1},{4,6},{5,7},{6,4},{7,5},{8,10},{9,11},{10,... | collective-permute-start | bytes 737288 | tf_op jit(solution)/shard_map/ppermute | solution.py:302
  34.9 48.5 %collective-permute-start.5 = (f32[480,128]{1,0:T(8,128)}, f32[480,128]{1,0:T(8,128)S(1)}, u32[]{:S(2)}, u32[]{:S(2)}) collective-permute-start(f32[480,128]{1,0:T(8,128)} %get-tuple-element.33), channel_id=1, source_target_pairs={{0,1},{1,0},{2,3},{3,2},{4,5},{5,4},{6,7},{7,6},{8,9},{9,8},{10,11... | collective-permute-start | bytes 737288 | tf_op jit(solution)/shard_map/ppermute | solution.py:302
  41.0 42.4 %collective-permute-start.6 = (f32[480,128]{1,0:T(8,128)}, f32[480,128]{1,0:T(8,128)S(1)}, u32[]{:S(2)}, u32[]{:S(2)}) collective-permute-start(f32[480,128]{1,0:T(8,128)} %get-tuple-element.34), channel_id=1, source_target_pairs={{0,3},{1,2},{2,1},{3,0},{4,7},{5,6},{6,5},{7,4},{8,11},{9,10},{10,... | collective-permute-start | bytes 737288 | tf_op jit(solution)/shard_map/ppermute | solution.py:302
  42.9 5.3 %copy-start.3 = (s32[8,4]{0,1:T(4,128)S(1)}, s32[8,4]{0,1:T(4,128)}, u32[]{:S(2)}) copy-start(s32[8,4]{0,1:T(4,128)} %param.8) | copy-start | bytes 388
  43.0 5.3 %copy-start.1 = (s32[8,4]{0,1:T(4,128)S(1)}, s32[8,4]{0,1:T(4,128)}, u32[]{:S(2)}) copy-start(s32[8,4]{0,1:T(4,128)} %param.9) | copy-start | bytes 388
  43.0 5.1 %collective-permute-start.2 = (f32[12,4,128]{2,1,0:T(4,128)S(1)}, f32[12,4,128]{2,1,0:T(4,128)S(1)}, u32[]{:S(2)}, u32[]{:S(2)}) collective-permute-start(f32[12,4,128]{2,1,0:T(4,128)S(1)} %get-tuple-element.26), channel_id=1, source_target_pairs={{128,256},{384,512},{640,768},{896,0},{256,128},{512,384},{768,640... | collective-permute-start | bytes 73736 | tf_op jit(solution)/shard_map/ppermute | solution.py:314
  44.9 3.3 %collective-permute-start.3 = (f32[12,4,128]{2,1,0:T(4,128)S(1)}, f32[12,4,128]{2,1,0:T(4,128)S(1)}, u32[]{:S(2)}, u32[]{:S(2)}) collective-permute-start(f32[12,4,128]{2,1,0:T(4,128)S(1)} %get-tuple-element.27), channel_id=1, source_target_pairs={{0,128},{256,384},{512,640},{768,896},{128,0},{384,256},{640,512},... | collective-permute-start | bytes 73736 | tf_op jit(solution)/shard_map/ppermute | solution.py:315
  48.2 0.9 copy-start
  51.0 32.4 %copy-start.2 = (f32[8,8]{1,0:T(8,128)S(1)}, f32[8,8]{1,0:T(8,128)}, u32[]{:S(2)}) copy-start(f32[8,8]{1,0:T(8,128)} %mix_ref.1) | copy-start | bytes 772
